TPU v7x, 32 devices: a whole 2x2x4 slice. The times are simulated.
32 devices in a mesh: parts: 2 (over x), seq: 16 (over z, y, core).
Axes of the slice: x: 2, y: 2, z: 4, core: 2. Of those that a mesh axis runs over, the one named last changes fastest.
Arguments:
- queries: bfloat16 [4096, 1024], P(('parts', 'seq')), parts along dimension 0, may hold values from -6 to 6
- keys: bfloat16 [4096, 1024], P(('parts', 'seq')), parts along dimension 0, may hold values from -6 to 6
- values: bfloat16 [4096, 1024], P(('parts', 'seq')), parts along dimension 0, may hold values from -6 to 6
- out_grads: bfloat16 [4096, 1024], P(('parts', 'seq')), parts along dimension 0, may hold values from -6 to 6
Outputs:
- query_out: bfloat16 [4096, 1024], P(('parts', 'seq')), parts along dimension 0
- key_out: bfloat16 [4096, 1024], P(('parts', 'seq')), parts along dimension 0
- value_out: bfloat16 [4096, 1024], P(('parts', 'seq')), parts along dimension 0
There are 2 independent parts, one for each index of `parts`. A program takes and returns all parts, laid end to end along the dimension named above; each array names one. Nothing has to cross between parts.
All inputs are finite; a program needn't handle non-finite values.
Results may differ from a plain program's by a relative error of at most 0.0049.
Values sent between devices are 32-bit elements; how exact they have to be, the bound alone decides.
No kernel may reach another device: no remote copies, remote signals or barrier semaphores. Data moves between devices by JAX's collectives and lax.ppermute only.
A program may use at most 192 MiB of HBM per device.

v0:
```python
import math

import jax
import jax.numpy as jnp
from jax import lax
from jax.sharding import PartitionSpec as P

HEADS = 8
HEAD_DIM = 128
GROUP = 128


def prefix(part, axis, combine, identity, reverse):
    count = lax.axis_size(axis)
    place = lax.axis_index(axis)
    ahead = count - 1 - place if reverse else place
    gathered = lax.all_gather(part, axis)
    state = jnp.zeros_like(part) + jnp.asarray(identity, part.dtype)

    def one(step, state):
        source = count - 1 - step if reverse else step
        return combine(state, lax.dynamic_index_in_dim(gathered, source, 0, False))

    return lax.fori_loop(0, ahead, one, state)


def add_states(first, second):
    return first + second


def local(queries, keys, values, out_grads):
    row_count = queries.shape[0]
    group_count = row_count // GROUP
    devices = lax.axis_size("seq")
    factor = 1.0 / math.sqrt(HEAD_DIM * row_count * devices)
    query_b = queries.reshape(group_count, GROUP, HEADS, HEAD_DIM)
    key_b = keys.reshape(group_count, GROUP, HEADS, HEAD_DIM)
    value_b = values.reshape(group_count, GROUP, HEADS, HEAD_DIM)
    grad_b = out_grads.reshape(group_count, GROUP, HEADS, HEAD_DIM)
    key_value = jnp.einsum("ncha,nchb->nhab", key_b, value_b, preferred_element_type=jnp.float32)
    query_grad = jnp.einsum("ncha,nchb->nhab", query_b, grad_b, preferred_element_type=jnp.float32)
    kv_totals = jnp.sum(key_value, 0)
    qg_totals = jnp.sum(query_grad, 0)
    empty_state = jnp.zeros((HEADS, HEAD_DIM, HEAD_DIM), jnp.float32)
    positions = jnp.arange(GROUP)
    causal = positions[None, :] <= positions[:, None]
    local_before = jnp.concatenate([empty_state[None], jnp.cumsum(key_value, 0)[:-1]], 0)
    local_after = jnp.concatenate([jnp.cumsum(query_grad[::-1], 0)[::-1][1:], empty_state[None]], 0)
    carried_before = prefix(kv_totals, "seq", add_states, empty_state, False)
    carried_after = prefix(qg_totals, "seq", add_states, empty_state, True)
    earlier = (carried_before[None] + local_before).astype(jnp.bfloat16)
    grad_scores = jnp.einsum("nchb,nshb->nhcs", grad_b, value_b, preferred_element_type=jnp.float32)
    grad_scores = jnp.where(causal, grad_scores, 0.0).astype(jnp.bfloat16)
    query_out = jnp.einsum(
        "nhcs,nsha->ncha", grad_scores, key_b, preferred_element_type=jnp.float32
    )
    query_out = query_out + jnp.einsum(
        "nchb,nhab->ncha", grad_b, earlier, preferred_element_type=jnp.float32
    )
    future = (carried_after[None] + local_after).astype(jnp.bfloat16)
    scores = jnp.einsum("ncha,nsha->nhcs", query_b, key_b, preferred_element_type=jnp.float32)
    scores = jnp.where(causal, scores, 0.0).astype(jnp.bfloat16)
    key_out = jnp.einsum(
        "nhcs,ncha->nsha", grad_scores, query_b, preferred_element_type=jnp.float32
    )
    key_out = key_out + jnp.einsum(
        "nshb,nhab->nsha", value_b, future, preferred_element_type=jnp.float32
    )
    value_out = jnp.einsum("nhcs,nchb->nshb", scores, grad_b, preferred_element_type=jnp.float32)
    value_out = value_out + jnp.einsum(
        "nsha,nhab->nshb", key_b, future, preferred_element_type=jnp.float32
    )

    def finish(array):
        return (factor * array).reshape(row_count, HEADS * HEAD_DIM).astype(jnp.bfloat16)

    return (finish(query_out), finish(key_out), finish(value_out))


def solution(mesh):
    return jax.shard_map(
        local,
        mesh=mesh,
        in_specs=(
            P(("parts", "seq"), None),
            P(("parts", "seq"), None),
            P(("parts", "seq"), None),
            P(("parts", "seq"), None),
        ),
        out_specs=(P(("parts", "seq"), None), P(("parts", "seq"), None), P(("parts", "seq"), None)),
        check_vma=False,
    )
```

profile of v0, /device:TPU:29, one launch (start us, length us, event | category | flops | bytes accessed | tf_op | source)
XLA Modules:
  0.0 188.3 jit_solution(18425347732369007380)
XLA Ops:
  7.2 1.2 copy.41
  8.4 2.1 %fusion.11 = f32[8,128,128]{2,1,0:T(8,128)} fusion(bf16[128,8,128]{0,2,1:T(8,128)(2,1)S(1)} %bitcast.116, bf16[128,1024]{1,0:T(8,128)(2,1)} %param.8), kind=kOutput, calls=%fused_computation.18 | convolution fusion | flops 33554432 | bytes 1048576 | tf_op jit(solution)/shard_map/ncha,nchb->nhab/dot_general | solution.py:41
  10.5 0.0 all-gather.5.cloned.1.call-start
  10.6 2.0 %fusion.18 = f32[8,128,128]{2,1,0:T(8,128)} fusion(bf16[128,1024]{1,0:T(8,128)(2,1)S(1)} %copy-done, bf16[128,1024]{1,0:T(8,128)(2,1)} %param.10), kind=kOutput, calls=%fused_computation.23 | convolution fusion | flops 33554432 | bytes 1048576 | tf_op jit(solution)/shard_map/ncha,nchb->nhab/dot_general | solution.py:40
  12.6 1.3 fusion.9
  13.9 70.4 %all-gather.7.cloned.1.call-done = f32[128,128,128]{2,1,0:T(8,128)} async-done(((f32[8,128,128]{2,1,0:T(8,128)}), f32[128,128,128]{2,1,0:T(8,128)}) %all-gather.7.cloned.1.call-update) | async-done | bytes 8388624 | tf_op jit(solution)/shard_map/all_gather | solution.py:17
  84.4 0.3 fusion.23
  84.7 0.3 fusion.21
  85.0 74.6 %all-gather.5.cloned.1.call-done = f32[128,128,128]{2,1,0:T(8,128)} async-done(((f32[8,128,128]{2,1,0:T(8,128)}), f32[128,128,128]{2,1,0:T(8,128)}) %all-gather.5.cloned.1.call-update) | async-done | bytes 8388624 | tf_op jit(solution)/shard_map/all_gather | solution.py:17
  159.7 17.9 %while.22 = (s32[]{:T(128)}, f32[8,128,128]{2,1,0:T(8,128)S(1)}, s32[]{:T(128)}, f32[16,8,128,128]{3,2,1,0:T(8,128)}, s32[]{:T(128)}, /*index=5*/s32[]{:T(128)}, s32[]{:T(128)}) while((s32[]{:T(128)}, f32[8,128,128]{2,1,0:T(8,128)S(1)}, s32[]{:T(128)}, f32[16,8,128,128]{3,2,1,0:T(8,128)}, s32[]{:T(128)}, /*index=5*/s32[]{:T(128)}, ...), condition=%wide.region_1.0_spmd, body=%wide.region_0.0_spmd.sunk | while | flops 131077 | bytes 1572987 | solution.py:24
  159.7 1.2 bitcast_add_fusion.4
  160.9 1.2 bitcast_add_fusion.4
  162.1 1.2 bitcast_add_fusion.4
  163.3 1.2 bitcast_add_fusion.4
  164.5 1.2 bitcast_add_fusion.4
  165.6 1.2 bitcast_add_fusion.4
  166.8 1.2 bitcast_add_fusion.4
  168.0 1.2 bitcast_add_fusion.4
  169.2 1.2 bitcast_add_fusion.4
  170.4 1.2 bitcast_add_fusion.4
  171.6 1.2 bitcast_add_fusion.4
  172.8 1.2 bitcast_add_fusion.4
  174.0 1.2 bitcast_add_fusion.4
  175.2 1.2 bitcast_add_fusion.4
  176.4 1.2 bitcast_add_fusion.4
  177.5 0.2 fusion.27
  177.8 0.3 fusion.8
  178.1 0.9 copy.36
  179.0 0.3 fusion.7
  179.2 0.8 copy.37
  180.1 0.5 fusion.6
  180.6 0.8 copy.38
  (13 shorter events, 0.2 us)
Async XLA Ops:
  7.2 3.4 %copy-start = (bf16[128,1024]{1,0:T(8,128)(2,1)S(1)}, bf16[128,1024]{1,0:T(8,128)(2,1)}, u32[]{:S(2)}) copy-start(bf16[128,1024]{1,0:T(8,128)(2,1)} %param.9) | copy-start | bytes 786436
  7.2 77.2 %copy-start.2 = (bf16[128,1024]{1,0:T(8,128)(2,1)S(1)}, bf16[128,1024]{1,0:T(8,128)(2,1)}, u32[]{:S(2)}) copy-start(bf16[128,1024]{1,0:T(8,128)(2,1)} %param.10) | copy-start | bytes 786436
  7.2 77.1 %all-gather.7.cloned.1.call-start = ((), (), s32[]{:S(2)}) async-start(), calls=%async_computation.1 | async-start | bytes 8912896 | tf_op jit(solution)/shard_map/all_gather | solution.py:17
  10.5 149.1 %all-gather.5.cloned.1.call-start = ((), (), s32[]{:S(2)}) async-start(), calls=%async_computation | async-start | bytes 8912896 | tf_op jit(solution)/shard_map/all_gather | solution.py:17
  84.3 94.6 %copy-start.1 = (bf16[128,1024]{1,0:T(8,128)(2,1)S(1)}, bf16[128,1024]{1,0:T(8,128)(2,1)}, u32[]{:S(2)}) copy-start(bf16[128,1024]{1,0:T(8,128)(2,1)} %param.8) | copy-start | bytes 786436
Sparse Core Ops, SparseCore 0:
  10.6 73.6 all-gather.6
  86.5 73.1 all-gather.4
where the time goes:
time: 189 us; the launch traced here: 188 us
  waiting for transfers between devices  145 us (77%)
  other arithmetic  17.6 us (9%)
  between operations  14.1 us (7%)
  matrix products  7.31 us (4%)
  local copies, waits for them, and re-layouts  3.81 us (2%)
    all_gather x2, waiting for transfers between devices, prefix(): gathered = lax.all_gather(part, axis)  145 us
    add x15, other arithmetic, add_states(): return first + second  17.5 us
  transfers between devices with their start and end apart: 2, of which 2 were waited for; matrix products, arithmetic and copies ran while one was open for 2% of the time, Pallas kernels for 0%

commit v1 on v0

v1 whole, which is shorter than its diff:
```python
import math

import jax
import jax.numpy as jnp
from jax import lax
from jax.experimental import pallas as pl
from jax.experimental.pallas import tpu as pltpu
from jax.sharding import PartitionSpec as P

HEADS = 8
HEAD_DIM = 128
GROUP = 128
AXIS = "seq"
VMEM = pl.BlockSpec(memory_space=pltpu.VMEM)


def place():
    index = lax.axis_index(AXIS)
    square = index >> 3
    return index & 1, (index >> 1) & 3, square, (square & 1) == 0


def swap(x, mask):
    count = lax.axis_size(AXIS)
    return lax.ppermute(x, AXIS, [(i, i ^ mask) for i in range(count)])


def columns(head):
    return pl.ds(pl.multiple_of(head * HEAD_DIM, HEAD_DIM), HEAD_DIM)


def dot(a, b, dims):
    return lax.dot_general(a, b, (dims, ((), ())), preferred_element_type=jnp.float32)


def states_kernel(first, q_ref, k_ref, v_ref, g_ref, keep_ref, send_ref):
    core, chip, _, even = place()
    pick = even if first else jnp.logical_not(even)

    def run(x_ref, y_ref):
        for half, out in ((1, send_ref), (0, keep_ref)):
            for slot in range(4):
                cols = columns(4 * (core ^ half) + (chip ^ slot))
                out[slot] = dot(x_ref[:, cols], y_ref[:, cols], ((0,), (0,)))

    pl.when(pick)(lambda: run(k_ref, v_ref))
    pl.when(jnp.logical_not(pick))(lambda: run(q_ref, g_ref))


def states(first, args):
    out = jax.ShapeDtypeStruct((4, HEAD_DIM, HEAD_DIM), jnp.float32)
    return pl.pallas_call(
        lambda *refs: states_kernel(first, *refs),
        out_shape=(out, out),
        in_specs=[VMEM] * 4,
        out_specs=(VMEM, VMEM),
        cost_estimate=pl.CostEstimate(flops=2 * 8 * 128**3, bytes_accessed=2**20, transcendentals=0),
        name="states",
    )(*args)


def inner_kernel(q_ref, k_ref, v_ref, g_ref, qo_ref, ko_ref, vo_ref):
    row = lax.broadcasted_iota(jnp.int32, (GROUP, GROUP), 0)
    col = lax.broadcasted_iota(jnp.int32, (GROUP, GROUP), 1)
    causal = col <= row
    for head in range(HEADS):
        cols = slice(head * HEAD_DIM, (head + 1) * HEAD_DIM)
        q, k, v, g = q_ref[:, cols], k_ref[:, cols], v_ref[:, cols], g_ref[:, cols]
        scores = jnp.where(causal, dot(q, k, ((1,), (1,))), 0.0).astype(jnp.bfloat16)
        grads = jnp.where(causal, dot(g, v, ((1,), (1,))), 0.0).astype(jnp.bfloat16)
        qo_ref[:, cols] = dot(grads, k, ((1,), (0,)))
        ko_ref[:, cols] = dot(grads, q, ((0,), (0,)))
        vo_ref[:, cols] = dot(scores, g, ((0,), (0,)))


def inner(args):
    out = jax.ShapeDtypeStruct(args[0].shape, jnp.float32)
    return pl.pallas_call(
        inner_kernel,
        out_shape=(out, out, out),
        in_specs=[VMEM] * 4,
        out_specs=(VMEM,) * 3,
        cost_estimate=pl.CostEstimate(flops=5 * 2 * 8 * 128**3, bytes_accessed=2**20, transcendentals=0),
        name="inner",
    )(*args)


def final_kernel(factor, k_ref, v_ref, g_ref, qi_ref, ki_ref, vi_ref, *refs):
    blocks, (qo_ref, ko_ref, vo_ref) = refs[:4], refs[4:]
    core, chip, _, even = place()
    own_a, own_b, other_a, other_b = blocks

    def run(flip):
        for half, a_ref, b_ref in ((0, own_a, own_b), (1, other_a, other_b)):
            earlier_ref, future_ref = (b_ref, a_ref) if flip else (a_ref, b_ref)
            for slot in range(4):
                cols = columns(4 * (core ^ half) + (chip ^ slot))
                earlier = earlier_ref[slot].astype(jnp.bfloat16)
                future = future_ref[slot].astype(jnp.bfloat16)
                qo = qi_ref[:, cols] + dot(g_ref[:, cols], earlier, ((1,), (1,)))
                ko = ki_ref[:, cols] + dot(v_ref[:, cols], future, ((1,), (1,)))
                vo = vi_ref[:, cols] + dot(k_ref[:, cols], future, ((1,), (0,)))
                qo_ref[:, cols] = (factor * qo).astype(jnp.bfloat16)
                ko_ref[:, cols] = (factor * ko).astype(jnp.bfloat16)
                vo_ref[:, cols] = (factor * vo).astype(jnp.bfloat16)

    pl.when(even)(lambda: run(False))
    pl.when(jnp.logical_not(even))(lambda: run(True))


def final(factor, *args):
    out = jax.ShapeDtypeStruct(args[0].shape, jnp.bfloat16)
    return pl.pallas_call(
        lambda *refs: final_kernel(factor, *refs),
        out_shape=(out, out, out),
        in_specs=[VMEM] * len(args),
        out_specs=(VMEM,) * 3,
        name="final",
    )(*args)


def scan(parts, chip, forward):
    sums = []
    for m in range(4):
        total = None
        for k in range(4):
            if k != m:
                ahead = jnp.where(forward, (chip ^ k) < (chip ^ m), (chip ^ k) > (chip ^ m))
                part = jnp.where(ahead, parts[k], 0.0)
                total = part if total is None else total + part
        sums.append(total)
    return sums


def between_squares(sum_a, sum_b, square, even, squares):
    if squares == 2:
        return None, swap(sum_a, 8)
    kv, qg = jnp.where(even, sum_a, sum_b), jnp.where(even, sum_b, sum_a)
    before, after = jnp.zeros_like(kv), jnp.zeros_like(qg)
    half = 1
    while half < squares:
        upper = (square & half) != 0
        out = jnp.where(upper, after + qg, before + kv)
        got = jnp.zeros_like(out)
        for step in range(half):
            pairs = []
            for base in range(0, squares, 2 * half):
                low, high = base + half - 1, base + half
                for r in range(8):
                    pairs.append((8 * low + r, 8 * (high + step) + r))
                    pairs.append((8 * high + r, 8 * (low - step) + r))
            got = got + lax.ppermute(out, AXIS, pairs)
        before, after = jnp.where(upper, before + got, before), jnp.where(upper, after, after + got)
        half *= 2
    return jnp.where(even, before, after), jnp.where(even, after, before)


def local(*args):
    queries, keys, values, out_grads = args
    devices = lax.axis_size(AXIS)
    factor = 1.0 / math.sqrt(HEAD_DIM * queries.shape[0] * devices)
    core, chip, square, even = place()

    keep_a, send_a = states(True, args)
    got_a = swap(send_a, 1)
    keep_b, send_b = states(False, args)
    got_b = swap(send_b, 1)
    total_a, total_b = keep_a + got_a, keep_b + got_b

    parts_a, parts_b = [total_a[0]], [total_b[0]]
    for m in (1, 2, 3):
        parts_a.append(swap(total_a[m], 2 * m))
    for m in (1, 2, 3):
        parts_b.append(swap(total_b[m], 2 * m))
    ahead_a, ahead_b = between_squares(sum(parts_a[1:], parts_a[0]), sum(parts_b[1:], parts_b[0]), square, even, devices // 8)
    scan_a, scan_b = scan(parts_a, chip, even), scan(parts_b, chip, jnp.logical_not(even))
    if ahead_a is not None:
        scan_a = [s + ahead_a for s in scan_a]
    scan_b = [s + ahead_b for s in scan_b]

    both = [jnp.stack([a, b]) for a, b in zip(scan_a, scan_b)]
    back = [both[0]] + [swap(both[m], 2 * m) for m in (1, 2, 3)]
    chip_a = jnp.stack([x[0] for x in back])
    chip_b = jnp.stack([x[1] for x in back])
    last = (core == 1) == even
    own_a, own_b = jnp.where(last, chip_a + got_a, chip_a), jnp.where(last, chip_b, chip_b + got_b)
    pair_a, pair_b = jnp.where(last, chip_a, chip_a + keep_a), jnp.where(last, chip_b + keep_b, chip_b)
    other = swap(jnp.stack([pair_a, pair_b]), 1)

    inner_q, inner_k, inner_v = inner(args)
    return final(factor, keys, values, out_grads, inner_q, inner_k, inner_v, own_a, own_b, other[0], other[1])


def solution(mesh):
    spec = P(("parts", "seq"), None)
    return jax.shard_map(local, mesh=mesh, in_specs=(spec,) * 4, out_specs=(spec,) * 3, check_vma=False)
```

time: 189 us -> 39.6 us (0.21)
  the two profiles are of different devices: /device:TPU:29 before, /device:TPU:0 now
where the time goes in v1:
time: 39.6 us; the launch traced here: 39.3 us
  starting transfers between devices  15.2 us (38%)
  Pallas kernels  12.1 us (31%)
  waiting for transfers between devices  8.6 us (22%)
  other arithmetic  1.77 us (4%)
  local copies, waits for them, and re-layouts  0.91 us (2%)
  between operations  0.71 us (2%)
    ppermute x13, starting transfers between devices, swap(): return lax.ppermute(x, AXIS, [(i, i ^ mask) for i in range(count)])  15.2 us
    ppermute x13, waiting for transfers between devices, swap(): return lax.ppermute(x, AXIS, [(i, i ^ mask) for i in range(count)])  8.6 us
    pallas_call x2, Pallas kernels, states(): pl.pallas_call(lambda *refs: states_kernel(first, *refs), out_shape=(out,...  4.57 us
    pallas_call x1, Pallas kernels, inner(): pl.pallas_call(inner_kernel, out_shape=(out, out, out), in_specs=[VMEM] *...  4.19 us
    pallas_call x1, Pallas kernels, final(): pl.pallas_call(lambda *refs: final_kernel(factor, *refs), out_shape=(out,...  3.35 us
    another operation x3, other arithmetic, local(): other = swap(jnp.stack([pair_a, pair_b]), 1)  1.55 us
    squeeze x1, local copies, waits for them, and re-layouts, local(): other[1]  0.84 us
  transfers between devices with their start and end apart: 13, of which 8 were waited for; matrix products, arithmetic and copies ran while one was open for 1% of the time, Pallas kernels for 17%

profile of v1, /device:TPU:0, one launch (start us, length us, event | category | flops | bytes accessed | tf_op | source)
XLA Modules:
  0.0 39.3 jit_solution(14023516606139624350)
XLA Ops:
  0.6 2.3 %states.2 = (f32[4,128,128]{2,1,0:T(8,128)}, f32[4,128,128]{2,1,0:T(8,128)}) custom-call(bf16[128,1024]{1,0:T(8,128)(2,1)} %refs_0_.4, bf16[128,1024]{1,0:T(8,128)(2,1)} %refs_0_.5, bf16[128,1024]{1,0:T(8,128)(2,1)} %refs_1_.5, bf16[128,1024]{1,0:T(8,128)(2,1)} %refs_2_.5), custom_call_target="tpu_custom_call" | custom-call | flops 33554432 | bytes 1048576 | tf_op jit(solution)/shard_map/states/pallas_call | solution.py:52
  2.9 0.5 %collective-permute-start = (f32[4,128,128]{2,1,0:T(8,128)}, f32[4,128,128]{2,1,0:T(8,128)S(1)}, u32[]{:S(2)}, u32[]{:S(2)}) collective-permute-start(f32[4,128,128]{2,1,0:T(8,128)} %get-tuple-element.14), channel_id=1, source_target_pairs={{0,1},{1,0},{2,3},{3,2},{4,5},{5,4},{6,7},{7,6},{8,9},{9,8},{10,11... | collective-permute-start | bytes 786440 | tf_op jit(solution)/shard_map/ppermute | solution.py:25
  3.4 2.3 %states.3 = (f32[4,128,128]{2,1,0:T(8,128)}, f32[4,128,128]{2,1,0:T(8,128)}) custom-call(bf16[128,1024]{1,0:T(8,128)(2,1)} %refs_0_.4, bf16[128,1024]{1,0:T(8,128)(2,1)} %refs_0_.5, bf16[128,1024]{1,0:T(8,128)(2,1)} %refs_1_.5, bf16[128,1024]{1,0:T(8,128)(2,1)} %refs_2_.5), custom_call_target="tpu_custom_call" | custom-call | flops 33554432 | bytes 1048576 | tf_op jit(solution)/shard_map/states/pallas_call | solution.py:52
  5.7 0.1 collective-permute-start.4
  5.7 0.0 collective-permute-done
  5.8 0.0 copy-start
  5.8 3.0 %collective-permute-start.1 = (f32[128,128]{1,0:T(8,128)S(1)}, f32[128,128]{1,0:T(8,128)S(1)}, u32[]{:S(2)}, u32[]{:S(2)}) collective-permute-start(f32[128,128]{1,0:T(8,128)S(1)} %get-tuple-element.34), channel_id=1, source_target_pairs={{0,2},{1,3},{2,0},{3,1},{4,6},{5,7},{6,4},{7,5},{8,10},{9,11},{10,... | collective-permute-start | bytes 196616 | tf_op jit(solution)/shard_map/ppermute | solution.py:25
  8.8 1.5 %collective-permute-start.3 = (f32[128,128]{1,0:T(8,128)S(1)}, f32[128,128]{1,0:T(8,128)S(1)}, u32[]{:S(2)}, u32[]{:S(2)}) collective-permute-start(f32[128,128]{1,0:T(8,128)S(1)} %get-tuple-element.35), channel_id=1, source_target_pairs={{0,6},{1,7},{2,4},{3,5},{4,2},{5,3},{6,0},{7,1},{8,14},{9,15},{10,... | collective-permute-start | bytes 196616 | tf_op jit(solution)/shard_map/ppermute | solution.py:25
  10.3 0.1 collective-permute-start.2
  10.5 3.0 %collective-permute-start.6 = (f32[128,128]{1,0:T(8,128)S(1)}, f32[128,128]{1,0:T(8,128)S(1)}, u32[]{:S(2)}, u32[]{:S(2)}) collective-permute-start(f32[128,128]{1,0:T(8,128)S(1)} %get-tuple-element.31), channel_id=1, source_target_pairs={{0,6},{1,7},{2,4},{3,5},{4,2},{5,3},{6,0},{7,1},{8,14},{9,15},{10,... | collective-permute-start | bytes 196616 | tf_op jit(solution)/shard_map/ppermute | solution.py:25
  13.4 0.5 %collective-permute-start.9 = (f32[128,128]{1,0:T(8,128)S(1)}, f32[128,128]{1,0:T(8,128)S(1)}, u32[]{:S(2)}, u32[]{:S(2)}) collective-permute-start(f32[128,128]{1,0:T(8,128)S(1)} %get-tuple-element.32), channel_id=1, source_target_pairs={{0,2},{1,3},{2,0},{3,1},{4,6},{5,7},{6,4},{7,5},{8,10},{9,11},{10,... | collective-permute-start | bytes 196616 | tf_op jit(solution)/shard_map/ppermute | solution.py:25
  14.0 0.1 collective-permute-start.5
  14.1 0.5 %collective-permute-done.3 = f32[128,128]{1,0:T(8,128)S(1)} collective-permute-done((f32[128,128]{1,0:T(8,128)S(1)}, f32[128,128]{1,0:T(8,128)S(1)}, u32[]{:S(2)}, u32[]{:S(2)}) %collective-permute-start.3) | collective-permute-done | bytes 65568 | tf_op jit(solution)/shard_map/ppermute | solution.py:25
  14.6 0.4 %collective-permute-done.2 = f32[128,128]{1,0:T(8,128)S(1)} collective-permute-done((f32[128,128]{1,0:T(8,128)S(1)}, f32[128,128]{1,0:T(8,128)S(1)}, u32[]{:S(2)}, u32[]{:S(2)}) %collective-permute-start.2) | collective-permute-done | bytes 65568 | tf_op jit(solution)/shard_map/ppermute | solution.py:25
  15.0 0.1 add_bitcast_fusion.3
  15.1 2.7 %collective-permute-start.7 = (f32[128,128]{1,0:T(8,128)S(1)}, f32[128,128]{1,0:T(8,128)S(1)}, u32[]{:S(2)}, u32[]{:S(2)}) collective-permute-start(f32[128,128]{1,0:T(8,128)S(1)} %get-tuple-element.20), channel_id=1, source_target_pairs={{0,8},{1,9},{2,10},{3,11},{4,12},{5,13},{6,14},{7,15},{8,0},{9,1},... | collective-permute-start | bytes 196616 | tf_op jit(solution)/shard_map/ppermute | solution.py:25
  17.8 0.1 collective-permute-done.9
  17.9 0.9 %collective-permute-done.5 = f32[128,128]{1,0:T(8,128)S(1)} collective-permute-done((f32[128,128]{1,0:T(8,128)S(1)}, f32[128,128]{1,0:T(8,128)S(1)}, u32[]{:S(2)}, u32[]{:S(2)}) %collective-permute-start.5) | collective-permute-done | bytes 65568 | tf_op jit(solution)/shard_map/ppermute | solution.py:25
  18.8 1.5 %collective-permute-done.7 = f32[128,128]{1,0:T(8,128)S(1)} collective-permute-done((f32[128,128]{1,0:T(8,128)S(1)}, f32[128,128]{1,0:T(8,128)S(1)}, u32[]{:S(2)}, u32[]{:S(2)}) %collective-permute-start.7) | collective-permute-done | bytes 65568 | tf_op jit(solution)/shard_map/ppermute | solution.py:25
  20.3 0.1 fusion.10
  20.4 1.4 %collective-permute-start.10 = (f32[2,128,128]{2,1,0:T(8,128)S(1)}, f32[2,128,128]{2,1,0:T(8,128)S(1)}, u32[]{:S(2)}, u32[]{:S(2)}) collective-permute-start(f32[2,128,128]{2,1,0:T(8,128)S(1)} %pad_maximum_fusion.4), channel_id=1, source_target_pairs={{0,4},{1,5},{2,6},{3,7},{4,0},{5,1},{6,2},{7,3},{8,12},{9,13},{10,... | collective-permute-start | bytes 393224 | tf_op jit(solution)/shard_map/ppermute | solution.py:25
  21.8 1.8 %collective-permute-start.11 = (f32[2,128,128]{2,1,0:T(8,128)S(1)}, f32[2,128,128]{2,1,0:T(8,128)S(1)}, u32[]{:S(2)}, u32[]{:S(2)}) collective-permute-start(f32[2,128,128]{2,1,0:T(8,128)S(1)} %pad_maximum_fusion.5), channel_id=1, source_target_pairs={{0,6},{1,7},{2,4},{3,5},{4,2},{5,3},{6,0},{7,1},{8,14},{9,15},{10,... | collective-permute-start | bytes 393224 | tf_op jit(solution)/shard_map/ppermute | solution.py:25
  23.6 0.5 %collective-permute-start.8 = (f32[2,128,128]{2,1,0:T(8,128)S(1)}, f32[2,128,128]{2,1,0:T(8,128)S(1)}, u32[]{:S(2)}, u32[]{:S(2)}) collective-permute-start(f32[2,128,128]{2,1,0:T(8,128)S(1)} %pad_maximum_fusion.3), channel_id=1, source_target_pairs={{0,2},{1,3},{2,0},{3,1},{4,6},{5,7},{6,4},{7,5},{8,10},{9,11},{10,... | collective-permute-start | bytes 393224 | tf_op jit(solution)/shard_map/ppermute | solution.py:25
  24.1 1.8 %collective-permute-done.10 = f32[2,128,128]{2,1,0:T(8,128)S(1)} collective-permute-done((f32[2,128,128]{2,1,0:T(8,128)S(1)}, f32[2,128,128]{2,1,0:T(8,128)S(1)}, u32[]{:S(2)}, u32[]{:S(2)}) %collective-permute-start.10) | collective-permute-done | bytes 131104 | tf_op jit(solution)/shard_map/ppermute | solution.py:25
  26.0 2.0 %collective-permute-done.11 = f32[2,128,128]{2,1,0:T(8,128)S(1)} collective-permute-done((f32[2,128,128]{2,1,0:T(8,128)S(1)}, f32[2,128,128]{2,1,0:T(8,128)S(1)}, u32[]{:S(2)}, u32[]{:S(2)}) %collective-permute-start.11) | collective-permute-done | bytes 131104 | tf_op jit(solution)/shard_map/ppermute | solution.py:25
  28.0 1.3 %collective-permute-done.8 = f32[2,128,128]{2,1,0:T(8,128)S(1)} collective-permute-done((f32[2,128,128]{2,1,0:T(8,128)S(1)}, f32[2,128,128]{2,1,0:T(8,128)S(1)}, u32[]{:S(2)}, u32[]{:S(2)}) %collective-permute-start.8) | collective-permute-done | bytes 131104 | tf_op jit(solution)/shard_map/ppermute | solution.py:25
  29.3 0.8 %fusion = (f32[1,4,128,128]{3,2,1,0:T(8,128)S(1)}, f32[4,128,128]{2,1,0:T(8,128)}) fusion(f32[4,128,128]{2,1,0:T(8,128)S(1)} %copy-done.1, f32[1,128,128]{2,1,0:T(8,128)S(1)} %get-tuple-element.43, f32[1,128,128]{2,1,0:T(8,128)S(1)} %get-tuple-element.41, f32[1,128,128]{2,1,0:T(8,128)S(1)} %get-tuple-element.39, f32[1,128,128]{2,1,0:T(8,128)S(1)} %get-tuple-element.37, ...), kind=kLoop, calls=%fused_computation.5 | loop fusion | flops 458752 | bytes 1310721 | tf_op jit(solution)/shard_map/stack | solution.py:188
  30.1 0.7 %fusion.1 = (f32[1,4,128,128]{3,2,1,0:T(8,128)S(1)}, f32[4,128,128]{2,1,0:T(8,128)}) fusion(f32[4,128,128]{2,1,0:T(8,128)S(1)} %copy-done, f32[1,128,128]{2,1,0:T(8,128)S(1)} %get-tuple-element.42, f32[1,128,128]{2,1,0:T(8,128)S(1)} %get-tuple-element.40, f32[1,128,128]{2,1,0:T(8,128)S(1)} %get-tuple-element.38, f32[1,128,128]{2,1,0:T(8,128)S(1)} %get-tuple-element.26, ...), kind=kLoop, calls=%fused_computation.6 | loop fusion | flops 458752 | bytes 1310721 | tf_op jit(solution)/shard_map/stack | solution.py:188
  30.9 0.1 collective-permute-start.12
  30.9 4.2 %inner.1 = (f32[128,1024]{1,0:T(8,128)}, f32[128,1024]{1,0:T(8,128)}, f32[128,1024]{1,0:T(8,128)}) custom-call(bf16[128,1024]{1,0:T(8,128)(2,1)} %refs_0_.4, bf16[128,1024]{1,0:T(8,128)(2,1)} %refs_0_.5, bf16[128,1024]{1,0:T(8,128)(2,1)} %refs_1_.5, bf16[128,1024]{1,0:T(8,128)(2,1)} %refs_2_.5), custom_call_target="tpu_custom_call" | custom-call | flops 167772160 | bytes 1048576 | tf_op jit(solution)/shard_map/inner/pallas_call | solution.py:78
  35.1 0.8 %slice_bitcast_fusion = (f32[4,128,128]{2,1,0:T(8,128)}, f32[4,128,128]{2,1,0:T(8,128)}) fusion(f32[2,4,128,128]{3,2,1,0:T(8,128)S(1)} %collective-permute-done.12), kind=kLoop, calls=%fused_computation.7 | loop fusion | bytes 1048576 | tf_op jit(solution)/shard_map/squeeze | solution.py:191
  36.0 3.4 %final.1 = (bf16[128,1024]{1,0:T(8,128)(2,1)}, bf16[128,1024]{1,0:T(8,128)(2,1)}, bf16[128,1024]{1,0:T(8,128)(2,1)}) custom-call(bf16[128,1024]{1,0:T(8,128)(2,1)} %refs_0_.5, bf16[128,1024]{1,0:T(8,128)(2,1)} %refs_1_.5, bf16[128,1024]{1,0:T(8,128)(2,1)} %refs_2_.5, f32[128,1024]{1,0:T(8,128)} %get-tuple-element.10.refs_3_, ...), custom_call_target="tpu_custom_call" | custom-call | tf_op jit(solution)/shard_map/final/pallas_call | solution.py:113
  (18 shorter events, 0.2 us)
Async XLA Ops:
  2.9 2.8 %collective-permute-start = (f32[4,128,128]{2,1,0:T(8,128)}, f32[4,128,128]{2,1,0:T(8,128)S(1)}, u32[]{:S(2)}, u32[]{:S(2)}) collective-permute-start(f32[4,128,128]{2,1,0:T(8,128)} %get-tuple-element.14), channel_id=1, source_target_pairs={{0,1},{1,0},{2,3},{3,2},{4,5},{5,4},{6,7},{7,6},{8,9},{9,8},{10,11... | collective-permute-start | bytes 786440 | tf_op jit(solution)/shard_map/ppermute | solution.py:25
  3.4 2.4 %copy-start.1 = (f32[4,128,128]{2,1,0:T(8,128)S(1)}, f32[4,128,128]{2,1,0:T(8,128)}, u32[]{:S(2)}) copy-start(f32[4,128,128]{2,1,0:T(8,128)} %get-tuple-element.13) | copy-start | bytes 786436
  5.7 4.7 %collective-permute-start.4 = (f32[4,128,128]{2,1,0:T(8,128)}, f32[4,128,128]{2,1,0:T(8,128)S(1)}, u32[]{:S(2)}, u32[]{:S(2)}) collective-permute-start(f32[4,128,128]{2,1,0:T(8,128)} %get-tuple-element.16), channel_id=1, source_target_pairs={{0,1},{1,0},{2,3},{3,2},{4,5},{5,4},{6,7},{7,6},{8,9},{9,8},{10,11... | collective-permute-start | bytes 786440 | tf_op jit(solution)/shard_map/ppermute | solution.py:25
  5.8 4.7 %copy-start = (f32[4,128,128]{2,1,0:T(8,128)S(1)}, f32[4,128,128]{2,1,0:T(8,128)}, u32[]{:S(2)}) copy-start(f32[4,128,128]{2,1,0:T(8,128)} %get-tuple-element.15) | copy-start | bytes 786436
  5.8 8.2 %collective-permute-start.1 = (f32[128,128]{1,0:T(8,128)S(1)}, f32[128,128]{1,0:T(8,128)S(1)}, u32[]{:S(2)}, u32[]{:S(2)}) collective-permute-start(f32[128,128]{1,0:T(8,128)S(1)} %get-tuple-element.34), channel_id=1, source_target_pairs={{0,2},{1,3},{2,0},{3,1},{4,6},{5,7},{6,4},{7,5},{8,10},{9,11},{10,... | collective-permute-start | bytes 196616 | tf_op jit(solution)/shard_map/ppermute | solution.py:25
  8.8 5.8 %collective-permute-start.3 = (f32[128,128]{1,0:T(8,128)S(1)}, f32[128,128]{1,0:T(8,128)S(1)}, u32[]{:S(2)}, u32[]{:S(2)}) collective-permute-start(f32[128,128]{1,0:T(8,128)S(1)} %get-tuple-element.35), channel_id=1, source_target_pairs={{0,6},{1,7},{2,4},{3,5},{4,2},{5,3},{6,0},{7,1},{8,14},{9,15},{10,... | collective-permute-start | bytes 196616 | tf_op jit(solution)/shard_map/ppermute | solution.py:25
  10.3 4.7 %collective-permute-start.2 = (f32[128,128]{1,0:T(8,128)S(1)}, f32[128,128]{1,0:T(8,128)S(1)}, u32[]{:S(2)}, u32[]{:S(2)}) collective-permute-start(f32[128,128]{1,0:T(8,128)S(1)} %get-tuple-element.36), channel_id=1, source_target_pairs={{0,4},{1,5},{2,6},{3,7},{4,0},{5,1},{6,2},{7,3},{8,12},{9,13},{10,... | collective-permute-start | bytes 196616 | tf_op jit(solution)/shard_map/ppermute | solution.py:25
  10.5 7.4 %collective-permute-start.6 = (f32[128,128]{1,0:T(8,128)S(1)}, f32[128,128]{1,0:T(8,128)S(1)}, u32[]{:S(2)}, u32[]{:S(2)}) collective-permute-start(f32[128,128]{1,0:T(8,128)S(1)} %get-tuple-element.31), channel_id=1, source_target_pairs={{0,6},{1,7},{2,4},{3,5},{4,2},{5,3},{6,0},{7,1},{8,14},{9,15},{10,... | collective-permute-start | bytes 196616 | tf_op jit(solution)/shard_map/ppermute | solution.py:25
  13.4 4.5 %collective-permute-start.9 = (f32[128,128]{1,0:T(8,128)S(1)}, f32[128,128]{1,0:T(8,128)S(1)}, u32[]{:S(2)}, u32[]{:S(2)}) collective-permute-start(f32[128,128]{1,0:T(8,128)S(1)} %get-tuple-element.32), channel_id=1, source_target_pairs={{0,2},{1,3},{2,0},{3,1},{4,6},{5,7},{6,4},{7,5},{8,10},{9,11},{10,... | collective-permute-start | bytes 196616 | tf_op jit(solution)/shard_map/ppermute | solution.py:25
  14.0 4.9 %collective-permute-start.5 = (f32[128,128]{1,0:T(8,128)S(1)}, f32[128,128]{1,0:T(8,128)S(1)}, u32[]{:S(2)}, u32[]{:S(2)}) collective-permute-start(f32[128,128]{1,0:T(8,128)S(1)} %get-tuple-element.33), channel_id=1, source_target_pairs={{0,4},{1,5},{2,6},{3,7},{4,0},{5,1},{6,2},{7,3},{8,12},{9,13},{10,... | collective-permute-start | bytes 196616 | tf_op jit(solution)/shard_map/ppermute | solution.py:25
  15.1 5.2 %collective-permute-start.7 = (f32[128,128]{1,0:T(8,128)S(1)}, f32[128,128]{1,0:T(8,128)S(1)}, u32[]{:S(2)}, u32[]{:S(2)}) collective-permute-start(f32[128,128]{1,0:T(8,128)S(1)} %get-tuple-element.20), channel_id=1, source_target_pairs={{0,8},{1,9},{2,10},{3,11},{4,12},{5,13},{6,14},{7,15},{8,0},{9,1},... | collective-permute-start | bytes 196616 | tf_op jit(solution)/shard_map/ppermute | solution.py:25
  20.4 5.5 %collective-permute-start.10 = (f32[2,128,128]{2,1,0:T(8,128)S(1)}, f32[2,128,128]{2,1,0:T(8,128)S(1)}, u32[]{:S(2)}, u32[]{:S(2)}) collective-permute-start(f32[2,128,128]{2,1,0:T(8,128)S(1)} %pad_maximum_fusion.4), channel_id=1, source_target_pairs={{0,4},{1,5},{2,6},{3,7},{4,0},{5,1},{6,2},{7,3},{8,12},{9,13},{10,... | collective-permute-start | bytes 393224 | tf_op jit(solution)/shard_map/ppermute | solution.py:25
  21.8 6.1 %collective-permute-start.11 = (f32[2,128,128]{2,1,0:T(8,128)S(1)}, f32[2,128,128]{2,1,0:T(8,128)S(1)}, u32[]{:S(2)}, u32[]{:S(2)}) collective-permute-start(f32[2,128,128]{2,1,0:T(8,128)S(1)} %pad_maximum_fusion.5), channel_id=1, source_target_pairs={{0,6},{1,7},{2,4},{3,5},{4,2},{5,3},{6,0},{7,1},{8,14},{9,15},{10,... | collective-permute-start | bytes 393224 | tf_op jit(solution)/shard_map/ppermute | solution.py:25
  23.6 5.7 %collective-permute-start.8 = (f32[2,128,128]{2,1,0:T(8,128)S(1)}, f32[2,128,128]{2,1,0:T(8,128)S(1)}, u32[]{:S(2)}, u32[]{:S(2)}) collective-permute-start(f32[2,128,128]{2,1,0:T(8,128)S(1)} %pad_maximum_fusion.3), channel_id=1, source_target_pairs={{0,2},{1,3},{2,0},{3,1},{4,6},{5,7},{6,4},{7,5},{8,10},{9,11},{10,... | collective-permute-start | bytes 393224 | tf_op jit(solution)/shard_map/ppermute | solution.py:25
  30.9 4.3 %collective-permute-start.12 = (f32[2,4,128,128]{3,2,1,0:T(8,128)S(1)}, f32[2,4,128,128]{3,2,1,0:T(8,128)S(1)}, u32[]{:S(2)}, u32[]{:S(2)}) collective-permute-start(f32[2,4,128,128]{3,2,1,0:T(8,128)S(1)} %pad_maximum_fusion), channel_id=1, source_target_pairs={{0,1},{1,0},{2,3},{3,2},{4,5},{5,4},{6,7},{7,6},{8,9},{9,8},{10,11... | collective-permute-start | bytes 1572872 | tf_op jit(solution)/shard_map/ppermute | solution.py:25

commit v2 on v1

--- a/solution.py
+++ b/solution.py
@@ -12,6 +12,8 @@
 GROUP = 128
 AXIS = "seq"
 VMEM = pl.BlockSpec(memory_space=pltpu.VMEM)
+HBM = pl.BlockSpec(memory_space=pltpu.HBM)
+PARAMS = pltpu.CompilerParams(vmem_limit_bytes=16 * 2**20)
 
 
 def place():
@@ -33,30 +35,44 @@
     return lax.dot_general(a, b, (dims, ((), ())), preferred_element_type=jnp.float32)
 
 
-def states_kernel(first, q_ref, k_ref, v_ref, g_ref, keep_ref, send_ref):
+def states_kernel(q_hbm, k_hbm, v_hbm, g_hbm, q_ref, k_ref, v_ref, g_ref, keep_a, send_a, keep_b, send_b, sems):
     core, chip, _, even = place()
-    pick = even if first else jnp.logical_not(even)
-
-    def run(x_ref, y_ref):
+    pairs = ((q_hbm, q_ref), (k_hbm, k_ref), (v_hbm, v_ref), (g_hbm, g_ref))
+    loads = [pltpu.make_async_copy(src, dst, sems.at[i]) for i, (src, dst) in enumerate(pairs)]
+    for load in loads:
+        load.start()
+    for load in loads:
+        load.wait()
+
+    def run(x_ref, y_ref, keep_ref, send_ref):
         for half, out in ((1, send_ref), (0, keep_ref)):
             for slot in range(4):
                 cols = columns(4 * (core ^ half) + (chip ^ slot))
                 out[slot] = dot(x_ref[:, cols], y_ref[:, cols], ((0,), (0,)))
 
-    pl.when(pick)(lambda: run(k_ref, v_ref))
-    pl.when(jnp.logical_not(pick))(lambda: run(q_ref, g_ref))
-
-
-def states(first, args):
+    @pl.when(even)
+    def _():
+        run(k_ref, v_ref, keep_a, send_a)
+        run(q_ref, g_ref, keep_b, send_b)
+
+    @pl.when(jnp.logical_not(even))
+    def _():
+        run(q_ref, g_ref, keep_a, send_a)
+        run(k_ref, v_ref, keep_b, send_b)
+
+
+def states(args):
+    rows = jax.ShapeDtypeStruct(args[0].shape, args[0].dtype)
     out = jax.ShapeDtypeStruct((4, HEAD_DIM, HEAD_DIM), jnp.float32)
     return pl.pallas_call(
-        lambda *refs: states_kernel(first, *refs),
-        out_shape=(out, out),
-        in_specs=[VMEM] * 4,
-        out_specs=(VMEM, VMEM),
-        cost_estimate=pl.CostEstimate(flops=2 * 8 * 128**3, bytes_accessed=2**20, transcendentals=0),
+        states_kernel,
+        out_shape=(rows,) * 4 + (out,) * 4,
+        in_specs=[HBM] * 4,
+        out_specs=(VMEM,) * 8,
+        scratch_shapes=[pltpu.SemaphoreType.DMA((4,))],
+        compiler_params=PARAMS,
         name="states",
-    )(*args)
+    )(*(pltpu.with_memory_space_constraint(x, pltpu.HBM) for x in args))
 
 
 def inner_kernel(q_ref, k_ref, v_ref, g_ref, qo_ref, ko_ref, vo_ref):
@@ -81,42 +97,50 @@
         in_specs=[VMEM] * 4,
         out_specs=(VMEM,) * 3,
         cost_estimate=pl.CostEstimate(flops=5 * 2 * 8 * 128**3, bytes_accessed=2**20, transcendentals=0),
+        compiler_params=PARAMS,
         name="inner",
     )(*args)
 
 
-def final_kernel(factor, k_ref, v_ref, g_ref, qi_ref, ki_ref, vi_ref, *refs):
-    blocks, (qo_ref, ko_ref, vo_ref) = refs[:4], refs[4:]
+def final_kernel(factor, half, k_ref, v_ref, g_ref, qi_ref, ki_ref, vi_ref, a_ref, b_ref, *refs):
+    qo_hbm, ko_hbm, vo_hbm, buffer, sems = refs[-5:]
     core, chip, _, even = place()
-    own_a, own_b, other_a, other_b = blocks
-
-    def run(flip):
-        for half, a_ref, b_ref in ((0, own_a, own_b), (1, other_a, other_b)):
-            earlier_ref, future_ref = (b_ref, a_ref) if flip else (a_ref, b_ref)
-            for slot in range(4):
-                cols = columns(4 * (core ^ half) + (chip ^ slot))
-                earlier = earlier_ref[slot].astype(jnp.bfloat16)
-                future = future_ref[slot].astype(jnp.bfloat16)
-                qo = qi_ref[:, cols] + dot(g_ref[:, cols], earlier, ((1,), (1,)))
-                ko = ki_ref[:, cols] + dot(v_ref[:, cols], future, ((1,), (1,)))
-                vo = vi_ref[:, cols] + dot(k_ref[:, cols], future, ((1,), (0,)))
-                qo_ref[:, cols] = (factor * qo).astype(jnp.bfloat16)
-                ko_ref[:, cols] = (factor * ko).astype(jnp.bfloat16)
-                vo_ref[:, cols] = (factor * vo).astype(jnp.bfloat16)
-
-    pl.when(even)(lambda: run(False))
-    pl.when(jnp.logical_not(even))(lambda: run(True))
-
-
-def final(factor, *args):
-    out = jax.ShapeDtypeStruct(args[0].shape, jnp.bfloat16)
+
+    def run(earlier_ref, future_ref):
+        for slot in range(4):
+            cols = columns(4 * (core ^ half) + (chip ^ slot))
+            earlier = earlier_ref[slot].astype(jnp.bfloat16)
+            future = future_ref[slot].astype(jnp.bfloat16)
+            qo = qi_ref[:, cols] + dot(g_ref[:, cols], earlier, ((1,), (1,)))
+            ko = ki_ref[:, cols] + dot(v_ref[:, cols], future, ((1,), (1,)))
+            vo = vi_ref[:, cols] + dot(k_ref[:, cols], future, ((1,), (0,)))
+            for i, value in enumerate((qo, ko, vo)):
+                buffer[i, slot] = (factor * value).astype(jnp.bfloat16)
+
+    pl.when(even)(lambda: run(a_ref, b_ref))
+    pl.when(jnp.logical_not(even))(lambda: run(b_ref, a_ref))
+    stores = []
+    for slot in range(4):
+        cols = columns(4 * (core ^ half) + (chip ^ slot))
+        for i, out in enumerate((qo_hbm, ko_hbm, vo_hbm)):
+            stores.append(pltpu.make_async_copy(buffer.at[i, slot], out.at[:, cols], sems.at[i, slot]))
+            stores[-1].start()
+    for store in stores:
+        store.wait()
+
+
+def final(factor, half, inputs, outs=()):
+    out = jax.ShapeDtypeStruct(inputs[0].shape, jnp.bfloat16)
     return pl.pallas_call(
-        lambda *refs: final_kernel(factor, *refs),
+        lambda *refs: final_kernel(factor, half, *refs),
         out_shape=(out, out, out),
-        in_specs=[VMEM] * len(args),
-        out_specs=(VMEM,) * 3,
+        in_specs=[VMEM] * len(inputs) + [HBM] * len(outs),
+        out_specs=(HBM,) * 3,
+        scratch_shapes=[pltpu.VMEM((3, 4, GROUP, HEAD_DIM), jnp.bfloat16), pltpu.SemaphoreType.DMA((3, 4))],
+        input_output_aliases={len(inputs) + i: i for i in range(len(outs))},
+        compiler_params=PARAMS,
         name="final",
-    )(*args)
+    )(*inputs, *outs)
 
 
 def scan(parts, chip, forward):
@@ -161,10 +185,11 @@
     factor = 1.0 / math.sqrt(HEAD_DIM * queries.shape[0] * devices)
     core, chip, square, even = place()
 
-    keep_a, send_a = states(True, args)
+    *args, keep_a, send_a, keep_b, send_b = states(args)
+    _, keys, values, out_grads = args
     got_a = swap(send_a, 1)
-    keep_b, send_b = states(False, args)
     got_b = swap(send_b, 1)
+    own_part = inner(args)
     total_a, total_b = keep_a + got_a, keep_b + got_b
 
     parts_a, parts_b = [total_a[0]], [total_b[0]]
@@ -180,6 +205,7 @@
 
     both = [jnp.stack([a, b]) for a, b in zip(scan_a, scan_b)]
     back = [both[0]] + [swap(both[m], 2 * m) for m in (1, 2, 3)]
+    back[3], own_part = lax.optimization_barrier((back[3], own_part))
     chip_a = jnp.stack([x[0] for x in back])
     chip_b = jnp.stack([x[1] for x in back])
     last = (core == 1) == even
@@ -187,8 +213,9 @@
     pair_a, pair_b = jnp.where(last, chip_a, chip_a + keep_a), jnp.where(last, chip_b + keep_b, chip_b)
     other = swap(jnp.stack([pair_a, pair_b]), 1)
 
-    inner_q, inner_k, inner_v = inner(args)
-    return final(factor, keys, values, out_grads, inner_q, inner_k, inner_v, own_a, own_b, other[0], other[1])
+    inputs = (keys, values, out_grads, *own_part)
+    outs = final(factor, 0, (*inputs, own_a, own_b))
+    return final(factor, 1, (*inputs, other[0], other[1]), outs)
 
 
 def solution(mesh):

time: 39.6 us -> 30.6 us (0.77)
  Pallas kernels: 12.1 us -> 5.95 us
  other arithmetic: 1.77 us -> 0.34 us
  waiting for transfers between devices: 8.6 us -> 7.77 us
  local copies, waits for them, and re-layouts: 0.91 us -> 0.09 us
  starting transfers between devices: 15.2 us -> 15.6 us
    pallas_call x3, Pallas kernels: 7.92 us -> 4.08 us  [the longest x2 2.38 us: final(): pl.pallas_call(lambda *refs: final_kernel(factor, half, *refs), out_shape...]
    pallas_call x1, Pallas kernels: 4.19 us -> 1.88 us  [inner(): pl.pallas_call(inner_kernel, out_shape=(out, out, out), in_specs=[VMEM] *...]
    another operation x3 -> x1, other arithmetic: 1.55 us -> 0.04 us  [local(): other = swap(jnp.stack([pair_a, pair_b]), 1)]
    ppermute x13, waiting for transfers between devices: 8.6 us -> 7.77 us  [swap(): return lax.ppermute(x, AXIS, [(i, i ^ mask) for i in range(count)])]
    squeeze x1, local copies, waits for them, and re-layouts: 0.84 us -> 0.03 us  [local(): return final(factor, 1, (*inputs, other[0], other[1]), outs)]
  transfers between devices with their start and end apart: 13 -> 13, of which waited for: 8 -> 7; matrix products, arithmetic and copies ran while one was open for 1% -> 1% of each run, Pallas kernels for 17% -> 10%
where the time goes in v2:
time: 30.6 us; the launch traced here: 30.5 us
  starting transfers between devices  15.6 us (51%)
  waiting for transfers between devices  7.77 us (25%)
  Pallas kernels  5.95 us (19%)
  between operations  0.77 us (3%)
  other arithmetic  0.34 us (1%)
    ppermute x13, starting transfers between devices, swap(): return lax.ppermute(x, AXIS, [(i, i ^ mask) for i in range(count)])  15.6 us
    ppermute x13, waiting for transfers between devices, swap(): return lax.ppermute(x, AXIS, [(i, i ^ mask) for i in range(count)])  7.77 us
    pallas_call x2, Pallas kernels, final(): pl.pallas_call(lambda *refs: final_kernel(factor, half, *refs), out_shape...  2.38 us
    pallas_call x1, Pallas kernels, inner(): pl.pallas_call(inner_kernel, out_shape=(out, out, out), in_specs=[VMEM] *...  1.88 us
    pallas_call x1, Pallas kernels, states(): pl.pallas_call(states_kernel, out_shape=(rows,) * 4 + (out,) * 4, in_spec...  1.7 us
  transfers between devices with their start and end apart: 13, of which 7 were waited for; matrix products, arithmetic and copies ran while one was open for 1% of the time, Pallas kernels for 10%

profile of v2, /device:TPU:0, one launch (start us, length us, event | category | flops | bytes accessed | tf_op | source)
XLA Modules:
  0.0 30.5 jit_solution(1588746811379981291)
XLA Ops:
  0.6 1.7 %states.1 = (bf16[128,1024]{1,0:T(8,128)(2,1)S(1)}, bf16[128,1024]{1,0:T(8,128)(2,1)S(1)}, bf16[128,1024]{1,0:T(8,128)(2,1)S(1)}, bf16[128,1024]{1,0:T(8,128)(2,...) custom-call(bf16[128,1024]{1,0:T(8,128)(2,1)} %q_hbm.1, ...), custom_call_target="tpu_custom_call" | custom-call | tf_op jit(solution)/shard_map/states/pallas_call | solution.py:67
  2.3 0.5 %collective-permute-start = (f32[4,128,128]{2,1,0:T(8,128)S(1)}, f32[4,128,128]{2,1,0:T(8,128)S(1)}, u32[]{:S(2)}, u32[]{:S(2)}) collective-permute-start(f32[4,128,128]{2,1,0:T(8,128)S(1)} %get-tuple-element.25), channel_id=1, source_target_pairs={{0,1},{1,0},{2,3},{3,2},{4,5},{5,4},{6,7},{7,6},{8,9},{9,8},{10,11... | collective-permute-start | bytes 786440 | tf_op jit(solution)/shard_map/ppermute | solution.py:27
  2.9 0.1 collective-permute-start.3
  2.9 1.1 %collective-permute-done = f32[4,128,128]{2,1,0:T(8,128)S(1)} collective-permute-done((f32[4,128,128]{2,1,0:T(8,128)S(1)}, f32[4,128,128]{2,1,0:T(8,128)S(1)}, u32[]{:S(2)}, u32[]{:S(2)}) %collective-permute-start) | collective-permute-done | bytes 262176 | tf_op jit(solution)/shard_map/ppermute | solution.py:27
  4.1 3.0 %collective-permute-start.1 = (f32[128,128]{1,0:T(8,128)S(1)}, f32[128,128]{1,0:T(8,128)S(1)}, u32[]{:S(2)}, u32[]{:S(2)}) collective-permute-start(f32[128,128]{1,0:T(8,128)S(1)} %get-tuple-element.56), channel_id=1, source_target_pairs={{0,2},{1,3},{2,0},{3,1},{4,6},{5,7},{6,4},{7,5},{8,10},{9,11},{10,... | collective-permute-start | bytes 196616 | tf_op jit(solution)/shard_map/ppermute | solution.py:27
  7.0 1.5 %collective-permute-start.6 = (f32[128,128]{1,0:T(8,128)S(1)}, f32[128,128]{1,0:T(8,128)S(1)}, u32[]{:S(2)}, u32[]{:S(2)}) collective-permute-start(f32[128,128]{1,0:T(8,128)S(1)} %get-tuple-element.57), channel_id=1, source_target_pairs={{0,6},{1,7},{2,4},{3,5},{4,2},{5,3},{6,0},{7,1},{8,14},{9,15},{10,... | collective-permute-start | bytes 196616 | tf_op jit(solution)/shard_map/ppermute | solution.py:27
  8.5 0.1 collective-permute-start.2
  8.6 0.0 collective-permute-done.3
  8.7 3.0 %collective-permute-start.9 = (f32[128,128]{1,0:T(8,128)S(1)}, f32[128,128]{1,0:T(8,128)S(1)}, u32[]{:S(2)}, u32[]{:S(2)}) collective-permute-start(f32[128,128]{1,0:T(8,128)S(1)} %get-tuple-element.53), channel_id=1, source_target_pairs={{0,6},{1,7},{2,4},{3,5},{4,2},{5,3},{6,0},{7,1},{8,14},{9,15},{10,... | collective-permute-start | bytes 196616 | tf_op jit(solution)/shard_map/ppermute | solution.py:27
  11.7 0.5 %collective-permute-start.5 = (f32[128,128]{1,0:T(8,128)S(1)}, f32[128,128]{1,0:T(8,128)S(1)}, u32[]{:S(2)}, u32[]{:S(2)}) collective-permute-start(f32[128,128]{1,0:T(8,128)S(1)} %get-tuple-element.54), channel_id=1, source_target_pairs={{0,4},{1,5},{2,6},{3,7},{4,0},{5,1},{6,2},{7,3},{8,12},{9,13},{10,... | collective-permute-start | bytes 196616 | tf_op jit(solution)/shard_map/ppermute | solution.py:27
  12.1 0.0 collective-permute-done.1
  12.1 0.6 %collective-permute-start.4 = (f32[128,128]{1,0:T(8,128)S(1)}, f32[128,128]{1,0:T(8,128)S(1)}, u32[]{:S(2)}, u32[]{:S(2)}) collective-permute-start(f32[128,128]{1,0:T(8,128)S(1)} %get-tuple-element.55), channel_id=1, source_target_pairs={{0,2},{1,3},{2,0},{3,1},{4,6},{5,7},{6,4},{7,5},{8,10},{9,11},{10,... | collective-permute-start | bytes 196616 | tf_op jit(solution)/shard_map/ppermute | solution.py:27
  12.7 0.0 collective-permute-done.6
  12.7 0.7 %collective-permute-done.2 = f32[128,128]{1,0:T(8,128)S(1)} collective-permute-done((f32[128,128]{1,0:T(8,128)S(1)}, f32[128,128]{1,0:T(8,128)S(1)}, u32[]{:S(2)}, u32[]{:S(2)}) %collective-permute-start.2) | collective-permute-done | bytes 65568 | tf_op jit(solution)/shard_map/ppermute | solution.py:27
  13.5 0.1 add_bitcast_fusion.2
  13.5 2.7 %collective-permute-start.7 = (f32[128,128]{1,0:T(8,128)S(1)}, f32[128,128]{1,0:T(8,128)S(1)}, u32[]{:S(2)}, u32[]{:S(2)}) collective-permute-start(f32[128,128]{1,0:T(8,128)S(1)} %get-tuple-element.42), channel_id=1, source_target_pairs={{0,8},{1,9},{2,10},{3,11},{4,12},{5,13},{6,14},{7,15},{8,0},{9,1},... | collective-permute-start | bytes 196616 | tf_op jit(solution)/shard_map/ppermute | solution.py:27
  16.2 1.9 %inner.1 = (f32[128,1024]{1,0:T(8,128)S(1)}, f32[128,1024]{1,0:T(8,128)S(1)}, f32[128,1024]{1,0:T(8,128)S(1)}) custom-call(bf16[128,1024]{1,0:T(8,128)(2,1)S(1)} %get-tuple-element.28.q_ref, bf16[128,1024]{1,0:T(8,128)(2,1)S(1)} %get-tuple-element.21.k_ref.refs_0_, bf16[128,1024]{1,0:T(8,128)(2,1)S(1)} %get-tuple-element.22.v_ref.refs_1_, ...), custom_call_target="tpu_custom_call" | custom-call | flops 167772160 | bytes 1048576 | tf_op jit(solution)/shard_map/inner/pallas_call | solution.py:94
  18.0 0.0 collective-permute-done.9
  18.1 0.0 collective-permute-done.5
  18.1 0.0 collective-permute-done.4
  18.1 1.4 %collective-permute-done.7 = f32[128,128]{1,0:T(8,128)S(1)} collective-permute-done((f32[128,128]{1,0:T(8,128)S(1)}, f32[128,128]{1,0:T(8,128)S(1)}, u32[]{:S(2)}, u32[]{:S(2)}) %collective-permute-start.7) | collective-permute-done | bytes 65568 | tf_op jit(solution)/shard_map/ppermute | solution.py:27
  19.4 0.1 fusion.7
  19.5 1.8 %collective-permute-start.8 = (f32[2,128,128]{2,1,0:T(8,128)S(1)}, f32[2,128,128]{2,1,0:T(8,128)S(1)}, u32[]{:S(2)}, u32[]{:S(2)}) collective-permute-start(f32[2,128,128]{2,1,0:T(8,128)S(1)} %pad_maximum_fusion.3), channel_id=1, source_target_pairs={{0,6},{1,7},{2,4},{3,5},{4,2},{5,3},{6,0},{7,1},{8,14},{9,15},{10,... | collective-permute-start | bytes 393224 | tf_op jit(solution)/shard_map/ppermute | solution.py:27
  21.3 0.7 %collective-permute-start.11 = (f32[2,128,128]{2,1,0:T(8,128)S(1)}, f32[2,128,128]{2,1,0:T(8,128)S(1)}, u32[]{:S(2)}, u32[]{:S(2)}) collective-permute-start(f32[2,128,128]{2,1,0:T(8,128)S(1)} %pad_maximum_fusion.5), channel_id=1, source_target_pairs={{0,4},{1,5},{2,6},{3,7},{4,0},{5,1},{6,2},{7,3},{8,12},{9,13},{10,... | collective-permute-start | bytes 393224 | tf_op jit(solution)/shard_map/ppermute | solution.py:27
  22.1 1.2 %collective-permute-start.10 = (f32[2,128,128]{2,1,0:T(8,128)S(1)}, f32[2,128,128]{2,1,0:T(8,128)S(1)}, u32[]{:S(2)}, u32[]{:S(2)}) collective-permute-start(f32[2,128,128]{2,1,0:T(8,128)S(1)} %pad_maximum_fusion.4), channel_id=1, source_target_pairs={{0,2},{1,3},{2,0},{3,1},{4,6},{5,7},{6,4},{7,5},{8,10},{9,11},{10,... | collective-permute-start | bytes 393224 | tf_op jit(solution)/shard_map/ppermute | solution.py:27
  23.2 2.2 %collective-permute-done.8 = f32[2,128,128]{2,1,0:T(8,128)S(1)} collective-permute-done((f32[2,128,128]{2,1,0:T(8,128)S(1)}, f32[2,128,128]{2,1,0:T(8,128)S(1)}, u32[]{:S(2)}, u32[]{:S(2)}) %collective-permute-start.8) | collective-permute-done | bytes 131104 | tf_op jit(solution)/shard_map/ppermute | solution.py:27
  25.5 0.9 %collective-permute-done.11 = f32[2,128,128]{2,1,0:T(8,128)S(1)} collective-permute-done((f32[2,128,128]{2,1,0:T(8,128)S(1)}, f32[2,128,128]{2,1,0:T(8,128)S(1)}, u32[]{:S(2)}, u32[]{:S(2)}) %collective-permute-start.11) | collective-permute-done | bytes 131104 | tf_op jit(solution)/shard_map/ppermute | solution.py:27
  26.4 0.7 %collective-permute-done.10 = f32[2,128,128]{2,1,0:T(8,128)S(1)} collective-permute-done((f32[2,128,128]{2,1,0:T(8,128)S(1)}, f32[2,128,128]{2,1,0:T(8,128)S(1)}, u32[]{:S(2)}, u32[]{:S(2)}) %collective-permute-start.10) | collective-permute-done | bytes 131104 | tf_op jit(solution)/shard_map/ppermute | solution.py:27
  27.3 0.1 collective-permute-start.12
  27.4 1.2 %final.2 = (bf16[128,1024]{1,0:T(8,128)(2,1)}, bf16[128,1024]{1,0:T(8,128)(2,1)}, bf16[128,1024]{1,0:T(8,128)(2,1)}) custom-call(bf16[128,1024]{1,0:T(8,128)(2,1)S(1)} %get-tuple-element.21.k_ref.refs_0_, bf16[128,1024]{1,0:T(8,128)(2,1)S(1)} %get-tuple-element.22.v_ref.refs_1_, bf16[128,1024]{1,0:T(8,128)(2,1)S(1)} %get-tuple-element.23.g_ref.refs_2_, ...), custom_call_target="tpu_custom_call" | custom-call | tf_op jit(solution)/shard_map/final/pallas_call | solution.py:134
  28.6 0.7 %collective-permute-done.12 = f32[2,4,128,128]{3,2,1,0:T(8,128)S(1)} collective-permute-done((f32[2,4,128,128]{3,2,1,0:T(8,128)S(1)}, f32[2,4,128,128]{3,2,1,0:T(8,128)S(1)}, u32[]{:S(2)}, u32[]{:S(2)}) %collective-permute-start.12) | collective-permute-done | bytes 524320 | tf_op jit(solution)/shard_map/ppermute | solution.py:27
  29.3 1.2 %final.3 = (bf16[128,1024]{1,0:T(8,128)(2,1)}, bf16[128,1024]{1,0:T(8,128)(2,1)}, bf16[128,1024]{1,0:T(8,128)(2,1)}) custom-call(bf16[128,1024]{1,0:T(8,128)(2,1)S(1)} %get-tuple-element.21.k_ref.refs_0_, bf16[128,1024]{1,0:T(8,128)(2,1)S(1)} %get-tuple-element.22.v_ref.refs_1_, ...), custom_call_target="tpu_custom_call", output_to_operand_aliasing={{0}: (8, {}), {1}: (9, {}), {2}: (10, {})} | custom-call | tf_op jit(solution)/shard_map/final/pallas_call | solution.py:134
  (14 shorter events, 0.3 us)
Async XLA Ops:
  2.3 1.7 %collective-permute-start = (f32[4,128,128]{2,1,0:T(8,128)S(1)}, f32[4,128,128]{2,1,0:T(8,128)S(1)}, u32[]{:S(2)}, u32[]{:S(2)}) collective-permute-start(f32[4,128,128]{2,1,0:T(8,128)S(1)} %get-tuple-element.25), channel_id=1, source_target_pairs={{0,1},{1,0},{2,3},{3,2},{4,5},{5,4},{6,7},{7,6},{8,9},{9,8},{10,11... | collective-permute-start | bytes 786440 | tf_op jit(solution)/shard_map/ppermute | solution.py:27
  2.9 5.8 %collective-permute-start.3 = (f32[4,128,128]{2,1,0:T(8,128)S(1)}, f32[4,128,128]{2,1,0:T(8,128)S(1)}, u32[]{:S(2)}, u32[]{:S(2)}) collective-permute-start(f32[4,128,128]{2,1,0:T(8,128)S(1)} %get-tuple-element.27), channel_id=1, source_target_pairs={{0,1},{1,0},{2,3},{3,2},{4,5},{5,4},{6,7},{7,6},{8,9},{9,8},{10,11... | collective-permute-start | bytes 786440 | tf_op jit(solution)/shard_map/ppermute | solution.py:27
  4.1 8.0 %collective-permute-start.1 = (f32[128,128]{1,0:T(8,128)S(1)}, f32[128,128]{1,0:T(8,128)S(1)}, u32[]{:S(2)}, u32[]{:S(2)}) collective-permute-start(f32[128,128]{1,0:T(8,128)S(1)} %get-tuple-element.56), channel_id=1, source_target_pairs={{0,2},{1,3},{2,0},{3,1},{4,6},{5,7},{6,4},{7,5},{8,10},{9,11},{10,... | collective-permute-start | bytes 196616 | tf_op jit(solution)/shard_map/ppermute | solution.py:27
  7.0 5.7 %collective-permute-start.6 = (f32[128,128]{1,0:T(8,128)S(1)}, f32[128,128]{1,0:T(8,128)S(1)}, u32[]{:S(2)}, u32[]{:S(2)}) collective-permute-start(f32[128,128]{1,0:T(8,128)S(1)} %get-tuple-element.57), channel_id=1, source_target_pairs={{0,6},{1,7},{2,4},{3,5},{4,2},{5,3},{6,0},{7,1},{8,14},{9,15},{10,... | collective-permute-start | bytes 196616 | tf_op jit(solution)/shard_map/ppermute | solution.py:27
  8.5 4.9 %collective-permute-start.2 = (f32[128,128]{1,0:T(8,128)S(1)}, f32[128,128]{1,0:T(8,128)S(1)}, u32[]{:S(2)}, u32[]{:S(2)}) collective-permute-start(f32[128,128]{1,0:T(8,128)S(1)} %get-tuple-element.58), channel_id=1, source_target_pairs={{0,4},{1,5},{2,6},{3,7},{4,0},{5,1},{6,2},{7,3},{8,12},{9,13},{10,... | collective-permute-start | bytes 196616 | tf_op jit(solution)/shard_map/ppermute | solution.py:27
  8.7 9.4 %collective-permute-start.9 = (f32[128,128]{1,0:T(8,128)S(1)}, f32[128,128]{1,0:T(8,128)S(1)}, u32[]{:S(2)}, u32[]{:S(2)}) collective-permute-start(f32[128,128]{1,0:T(8,128)S(1)} %get-tuple-element.53), channel_id=1, source_target_pairs={{0,6},{1,7},{2,4},{3,5},{4,2},{5,3},{6,0},{7,1},{8,14},{9,15},{10,... | collective-permute-start | bytes 196616 | tf_op jit(solution)/shard_map/ppermute | solution.py:27
  11.7 6.4 %collective-permute-start.5 = (f32[128,128]{1,0:T(8,128)S(1)}, f32[128,128]{1,0:T(8,128)S(1)}, u32[]{:S(2)}, u32[]{:S(2)}) collective-permute-start(f32[128,128]{1,0:T(8,128)S(1)} %get-tuple-element.54), channel_id=1, source_target_pairs={{0,4},{1,5},{2,6},{3,7},{4,0},{5,1},{6,2},{7,3},{8,12},{9,13},{10,... | collective-permute-start | bytes 196616 | tf_op jit(solution)/shard_map/ppermute | solution.py:27
  12.1 6.0 %collective-permute-start.4 = (f32[128,128]{1,0:T(8,128)S(1)}, f32[128,128]{1,0:T(8,128)S(1)}, u32[]{:S(2)}, u32[]{:S(2)}) collective-permute-start(f32[128,128]{1,0:T(8,128)S(1)} %get-tuple-element.55), channel_id=1, source_target_pairs={{0,2},{1,3},{2,0},{3,1},{4,6},{5,7},{6,4},{7,5},{8,10},{9,11},{10,... | collective-permute-start | bytes 196616 | tf_op jit(solution)/shard_map/ppermute | solution.py:27
  13.5 5.9 %collective-permute-start.7 = (f32[128,128]{1,0:T(8,128)S(1)}, f32[128,128]{1,0:T(8,128)S(1)}, u32[]{:S(2)}, u32[]{:S(2)}) collective-permute-start(f32[128,128]{1,0:T(8,128)S(1)} %get-tuple-element.42), channel_id=1, source_target_pairs={{0,8},{1,9},{2,10},{3,11},{4,12},{5,13},{6,14},{7,15},{8,0},{9,1},... | collective-permute-start | bytes 196616 | tf_op jit(solution)/shard_map/ppermute | solution.py:27
  19.5 5.9 %collective-permute-start.8 = (f32[2,128,128]{2,1,0:T(8,128)S(1)}, f32[2,128,128]{2,1,0:T(8,128)S(1)}, u32[]{:S(2)}, u32[]{:S(2)}) collective-permute-start(f32[2,128,128]{2,1,0:T(8,128)S(1)} %pad_maximum_fusion.3), channel_id=1, source_target_pairs={{0,6},{1,7},{2,4},{3,5},{4,2},{5,3},{6,0},{7,1},{8,14},{9,15},{10,... | collective-permute-start | bytes 393224 | tf_op jit(solution)/shard_map/ppermute | solution.py:27
  21.3 5.0 %collective-permute-start.11 = (f32[2,128,128]{2,1,0:T(8,128)S(1)}, f32[2,128,128]{2,1,0:T(8,128)S(1)}, u32[]{:S(2)}, u32[]{:S(2)}) collective-permute-start(f32[2,128,128]{2,1,0:T(8,128)S(1)} %pad_maximum_fusion.5), channel_id=1, source_target_pairs={{0,4},{1,5},{2,6},{3,7},{4,0},{5,1},{6,2},{7,3},{8,12},{9,13},{10,... | collective-permute-start | bytes 393224 | tf_op jit(solution)/shard_map/ppermute | solution.py:27
  22.1 5.0 %collective-permute-start.10 = (f32[2,128,128]{2,1,0:T(8,128)S(1)}, f32[2,128,128]{2,1,0:T(8,128)S(1)}, u32[]{:S(2)}, u32[]{:S(2)}) collective-permute-start(f32[2,128,128]{2,1,0:T(8,128)S(1)} %pad_maximum_fusion.4), channel_id=1, source_target_pairs={{0,2},{1,3},{2,0},{3,1},{4,6},{5,7},{6,4},{7,5},{8,10},{9,11},{10,... | collective-permute-start | bytes 393224 | tf_op jit(solution)/shard_map/ppermute | solution.py:27
  27.3 2.0 %collective-permute-start.12 = (f32[2,4,128,128]{3,2,1,0:T(8,128)S(1)}, f32[2,4,128,128]{3,2,1,0:T(8,128)S(1)}, u32[]{:S(2)}, u32[]{:S(2)}) collective-permute-start(f32[2,4,128,128]{3,2,1,0:T(8,128)S(1)} %pad_maximum_fusion), channel_id=1, source_target_pairs={{0,1},{1,0},{2,3},{3,2},{4,5},{5,4},{6,7},{7,6},{8,9},{9,8},{10,11... | collective-permute-start | bytes 1572872 | tf_op jit(solution)/shard_map/ppermute | solution.py:27

commit v3 on v2

v3 whole, which is shorter than its diff:
```python
import math

import jax
import jax.numpy as jnp
from jax import lax
from jax.experimental import pallas as pl
from jax.experimental.pallas import tpu as pltpu
from jax.sharding import PartitionSpec as P

HEADS = 8
HEAD_DIM = 128
GROUP = 128
AXIS = "seq"
VMEM = pl.BlockSpec(memory_space=pltpu.VMEM)
HBM = pl.BlockSpec(memory_space=pltpu.HBM)
PARAMS = pltpu.CompilerParams(vmem_limit_bytes=16 * 2**20)
PIECES = ((0, 3), (1, 2))


def place():
    index = lax.axis_index(AXIS)
    square = index >> 3
    return index & 1, (index >> 1) & 3, square, (square & 1) == 0


def swap(x, mask):
    count = lax.axis_size(AXIS)
    return lax.ppermute(x, AXIS, [(i, i ^ mask) for i in range(count)])


def columns(half, slot, core, chip):
    return pl.ds(pl.multiple_of((4 * (core ^ half) + (chip ^ slot)) * HEAD_DIM, HEAD_DIM), HEAD_DIM)


def dot(a, b, dims):
    return lax.dot_general(a, b, (dims, ((), ())), preferred_element_type=jnp.float32)


def heads(*count):
    return jax.ShapeDtypeStruct((*count, HEAD_DIM, HEAD_DIM), jnp.float32)


def in_vmem(kernel, out_shape, args, name):
    return pl.pallas_call(
        kernel,
        out_shape=out_shape,
        in_specs=[VMEM] * len(args),
        out_specs=jax.tree.map(lambda _: VMEM, out_shape),
        compiler_params=PARAMS,
        name=name,
    )(*args)


def write_states(x_ref, y_ref, out_ref, half, core, chip):
    for slot in range(4):
        cols = columns(half, slot, core, chip)
        out_ref[slot] = dot(x_ref[:, cols], y_ref[:, cols], ((0,), (0,)))


def first_kernel(q_hbm, k_hbm, v_hbm, g_hbm, q_ref, k_ref, v_ref, g_ref, send_ref, sems):
    core, chip, _, even = place()
    q, k, v, g = (
        pltpu.make_async_copy(src, dst, sems.at[i])
        for i, (src, dst) in enumerate(((q_hbm, q_ref), (k_hbm, k_ref), (v_hbm, v_ref), (g_hbm, g_ref)))
    )

    def run(now, later, x_ref, y_ref):
        for load in (*now, *later):
            load.start()
        for load in now:
            load.wait()
        write_states(x_ref, y_ref, send_ref, 1, core, chip)
        for load in later:
            load.wait()

    pl.when(even)(lambda: run((k, v), (q, g), k_ref, v_ref))
    pl.when(jnp.logical_not(even))(lambda: run((q, g), (k, v), q_ref, g_ref))


def first_states(args):
    rows = jax.ShapeDtypeStruct(args[0].shape, args[0].dtype)
    return pl.pallas_call(
        first_kernel,
        out_shape=(rows,) * 4 + (heads(4),),
        in_specs=[HBM] * 4,
        out_specs=(VMEM,) * 5,
        scratch_shapes=[pltpu.SemaphoreType.DMA((4,))],
        compiler_params=PARAMS,
        name="first_states",
    )(*(pltpu.with_memory_space_constraint(x, pltpu.HBM) for x in args))


def second_kernel(q_ref, k_ref, v_ref, g_ref, send_b, keep_a, keep_b):
    core, chip, _, even = place()

    def run(x_ref, y_ref, z_ref, w_ref):
        write_states(z_ref, w_ref, send_b, 1, core, chip)
        write_states(x_ref, y_ref, keep_a, 0, core, chip)
        write_states(z_ref, w_ref, keep_b, 0, core, chip)

    pl.when(even)(lambda: run(k_ref, v_ref, q_ref, g_ref))
    pl.when(jnp.logical_not(even))(lambda: run(q_ref, g_ref, k_ref, v_ref))


def inner_kernel(q_ref, k_ref, v_ref, g_ref, qo_ref, ko_ref, vo_ref):
    row = lax.broadcasted_iota(jnp.int32, (GROUP, GROUP), 0)
    col = lax.broadcasted_iota(jnp.int32, (GROUP, GROUP), 1)
    causal = col <= row
    for head in range(HEADS):
        cols = slice(head * HEAD_DIM, (head + 1) * HEAD_DIM)
        q, k, v, g = q_ref[:, cols], k_ref[:, cols], v_ref[:, cols], g_ref[:, cols]
        scores = jnp.where(causal, dot(q, k, ((1,), (1,))), 0.0).astype(jnp.bfloat16)
        grads = jnp.where(causal, dot(g, v, ((1,), (1,))), 0.0).astype(jnp.bfloat16)
        qo_ref[:, cols] = dot(grads, k, ((1,), (0,)))
        ko_ref[:, cols] = dot(grads, q, ((0,), (0,)))
        vo_ref[:, cols] = dot(scores, g, ((0,), (0,)))


def scan(parts, start, slot, chip, forward):
    total = start
    for k in range(4):
        if k != slot:
            use = jnp.where(forward, (chip ^ k) < (chip ^ slot), (chip ^ k) > (chip ^ slot))
            total = total + jnp.where(use, parts[k][...], 0.0)
    return total


def scan_a_kernel(*refs):
    parts, ahead, outs = refs[:4], refs[4:-4], refs[-4:]
    _, chip, _, even = place()
    for slot in range(4):
        start = ahead[0][...] if ahead else jnp.zeros((HEAD_DIM, HEAD_DIM), jnp.float32)
        outs[slot][...] = scan(parts, start, slot, chip, even)


def scan_b_kernel(*refs):
    scanned_a, parts, ahead, outs = refs[:4], refs[4:8], refs[8], refs[9:]
    _, chip, _, even = place()
    for slot in range(4):
        outs[slot][0] = scanned_a[slot][...]
        outs[slot][1] = scan(parts, ahead[...], slot, chip, jnp.logical_not(even))


def pair_kernel(slots, keep_a, keep_b, *refs):
    core, _, _, even = place()
    last = (core == 1) == even
    out = refs[-1]
    for n, slot in enumerate(slots):
        out[n, 0] = refs[n][0] + jnp.where(last, 0.0, keep_a[slot])
        out[n, 1] = refs[n][1] + jnp.where(last, keep_b[slot], 0.0)


def final_kernel(factor, half, k_ref, v_ref, g_ref, qi_ref, ki_ref, vi_ref, *refs):
    qo_hbm, ko_hbm, vo_hbm, buffer, sems = refs[-5:]
    core, chip, _, even = place()
    last = (core == 1) == even

    def total(slot, i):
        if half == 1:
            for ref, slots in zip(refs, PIECES):
                if slot in slots:
                    return ref[slots.index(slot), i].astype(jnp.bfloat16)
        use = last if i == 0 else jnp.logical_not(last)
        return (refs[slot][i] + jnp.where(use, refs[4 + i][slot], 0.0)).astype(jnp.bfloat16)

    stores = []
    for slot in (slot for slots in PIECES for slot in slots):
        cols = columns(half, slot, core, chip)
        a, b = total(slot, 0), total(slot, 1)
        earlier, future = jnp.where(even, a, b), jnp.where(even, b, a)
        qo = qi_ref[:, cols] + dot(g_ref[:, cols], earlier, ((1,), (1,)))
        ko = ki_ref[:, cols] + dot(v_ref[:, cols], future, ((1,), (1,)))
        vo = vi_ref[:, cols] + dot(k_ref[:, cols], future, ((1,), (0,)))
        for i, (value, out) in enumerate(((qo, qo_hbm), (ko, ko_hbm), (vo, vo_hbm))):
            buffer[i, slot] = (factor * value).astype(jnp.bfloat16)
            stores.append(pltpu.make_async_copy(buffer.at[i, slot], out.at[:, cols], sems.at[i, slot]))
            stores[-1].start()
    for store in stores:
        store.wait()


def final(factor, half, inputs, outs=()):
    out = jax.ShapeDtypeStruct(inputs[0].shape, jnp.bfloat16)
    return pl.pallas_call(
        lambda *refs: final_kernel(factor, half, *refs),
        out_shape=(out, out, out),
        in_specs=[VMEM] * len(inputs) + [HBM] * len(outs),
        out_specs=(HBM,) * 3,
        scratch_shapes=[pltpu.VMEM((3, 4, GROUP, HEAD_DIM), jnp.bfloat16), pltpu.SemaphoreType.DMA((3, 4))],
        input_output_aliases={len(inputs) + i: i for i in range(len(outs))},
        compiler_params=PARAMS,
        name="final",
    )(*inputs, *outs)


def between_squares(sum_a, sum_b, squares):
    if squares == 2:
        return [swap(sum_a, 8)]
    _, _, square, even = place()
    kv, qg = jnp.where(even, sum_a, sum_b), jnp.where(even, sum_b, sum_a)
    before, after = jnp.zeros_like(kv), jnp.zeros_like(qg)
    half = 1
    while half < squares:
        upper = (square & half) != 0
        out = jnp.where(upper, after + qg, before + kv)
        got = jnp.zeros_like(out)
        for step in range(half):
            pairs = []
            for base in range(0, squares, 2 * half):
                low, high = base + half - 1, base + half
                for r in range(8):
                    pairs.append((8 * low + r, 8 * (high + step) + r))
                    pairs.append((8 * high + r, 8 * (low - step) + r))
            got = got + lax.ppermute(out, AXIS, pairs)
        before, after = jnp.where(upper, before + got, before), jnp.where(upper, after, after + got)
        half *= 2
    return [jnp.where(even, before, after), jnp.where(even, after, before)]


def local(*args):
    devices = lax.axis_size(AXIS)
    factor = 1.0 / math.sqrt(HEAD_DIM * args[0].shape[0] * devices)

    *args, send_a = first_states(args)
    got_a = swap(send_a, 1)
    send_b, keep_a, keep_b = in_vmem(second_kernel, (heads(4),) * 3, args, "second_states")
    got_b = swap(send_b, 1)
    rows = jax.ShapeDtypeStruct(args[0].shape, jnp.float32)
    own_part = in_vmem(inner_kernel, (rows,) * 3, args, "inner")

    parts_a = [keep_a[0] + got_a[0]] + [swap(keep_a[m] + got_a[m], 2 * m) for m in (1, 2, 3)]
    parts_b = [keep_b[0] + got_b[0]] + [swap(keep_b[m] + got_b[m], 2 * m) for m in (1, 2, 3)]
    sum_a = parts_a[0]
    for m in (2, 3, 1):
        (sum_a,) = lax.optimization_barrier((sum_a + parts_a[m],))
    ahead = between_squares(sum_a, sum(parts_b[1:], parts_b[0]), devices // 8)
    scanned = in_vmem(scan_a_kernel, (heads(),) * 4, (*parts_a, *ahead[:-1]), "scan_a")
    scanned = in_vmem(scan_b_kernel, (heads(2),) * 4, (*scanned, *parts_b, ahead[-1]), "scan_b")
    back = [scanned[0]] + [swap(scanned[m], 2 * m) for m in (1, 2, 3)]
    back[1], own_part = lax.optimization_barrier((back[1], own_part))

    others = []
    for slots in PIECES:
        kernel = lambda *refs, slots=slots: pair_kernel(slots, *refs)
        pair = in_vmem(kernel, heads(len(slots), 2), (keep_a, keep_b, *(back[m] for m in slots)), "pair")
        others.append(swap(pair, 1))
    inputs = (*args[1:], *own_part)
    outs = final(factor, 0, (*inputs, *back, got_a, got_b))
    return final(factor, 1, (*inputs, *others), outs)


def solution(mesh):
    spec = P(("parts", "seq"), None)
    return jax.shard_map(local, mesh=mesh, in_specs=(spec,) * 4, out_specs=(spec,) * 3, check_vma=False)
```

time: 30.6 us -> 29.2 us (0.954)
  waiting for transfers between devices: 7.77 us -> 6.84 us
    ppermute x13 -> x14, waiting for transfers between devices: 7.77 us -> 6.84 us  [swap(): return lax.ppermute(x, AXIS, [(i, i ^ mask) for i in range(count)])]
    pallas_call x2 -> x7, Pallas kernels: 3.57 us -> 3.76 us  [the longest x6 2.46 us: in_vmem(): pl.pallas_call(kernel, out_shape=out_shape, in_specs=[VMEM] * len(args),...]
    ppermute x13 -> x14, starting transfers between devices: 15.6 us -> 15.5 us  [swap(): return lax.ppermute(x, AXIS, [(i, i ^ mask) for i in range(count)])]
  transfers between devices with their start and end apart: 13 -> 14, of which waited for: 7 -> 10; matrix products, arithmetic and copies ran while one was open for 1% -> 0% of each run, Pallas kernels for 10% -> 12%
where the time goes in v3:
time: 29.2 us; the launch traced here: 29.1 us
  starting transfers between devices  15.5 us (53%)
  waiting for transfers between devices  6.84 us (23%)
  Pallas kernels  5.93 us (20%)
  between operations  0.74 us (3%)
    ppermute x14, starting transfers between devices, swap(): return lax.ppermute(x, AXIS, [(i, i ^ mask) for i in range(count)])  15.5 us
    ppermute x14, waiting for transfers between devices, swap(): return lax.ppermute(x, AXIS, [(i, i ^ mask) for i in range(count)])  6.84 us
    pallas_call x6, Pallas kernels, in_vmem(): pl.pallas_call(kernel, out_shape=out_shape, in_specs=[VMEM] * len(args),...  2.46 us
    pallas_call x2, Pallas kernels, final(): pl.pallas_call(lambda *refs: final_kernel(factor, half, *refs), out_shape...  2.17 us
    pallas_call x1, Pallas kernels, first_states(): pl.pallas_call(first_kernel, out_shape=(rows,) * 4 + (heads(4),), in_spec...  1.3 us
  transfers between devices with their start and end apart: 14, of which 10 were waited for; matrix products, arithmetic and copies ran while one was open for 0% of the time, Pallas kernels for 12%

profile of v3, /device:TPU:0, one launch (start us, length us, event | category | flops | bytes accessed | tf_op | source)
XLA Modules:
  0.0 29.1 jit_solution(2726240861640583880)
XLA Ops:
  0.6 1.3 %first_states.1 = (bf16[128,1024]{1,0:T(8,128)(2,1)S(1)}, bf16[128,1024]{1,0:T(8,128)(2,1)S(1)}, bf16[128,1024]{1,0:T(8,128)(2,1)S(1)}, bf16[128,1024]{1,0:T(8,128)(2,1)S(1)}, f32[4,128,128]{2,1,0:T(8,128)S(1)}) custom-call(bf16[128,1024]{1,0:T(8,128)(2,1)} %q_hbm.1, bf16[128,1024]{1,0:T(8,128)(2,1)} %k_hbm.1, bf16[128,1024]{1,0:T(8,128)(2,1)} %v_hbm.1, ...), custom_call_target="tpu_custom_call" | custom-call | tf_op jit(solution)/shard_map/first_states/pallas_call | solution.py:82
  1.9 0.5 %collective-permute-start = (f32[4,128,128]{2,1,0:T(8,128)S(1)}, f32[4,128,128]{2,1,0:T(8,128)S(1)}, u32[]{:S(2)}, u32[]{:S(2)}) collective-permute-start(f32[4,128,128]{2,1,0:T(8,128)S(1)} %get-tuple-element.34), channel_id=1, source_target_pairs={{0,1},{1,0},{2,3},{3,2},{4,5},{5,4},{6,7},{7,6},{8,9},{9,8},{10,11... | collective-permute-start | bytes 786440 | tf_op jit(solution)/shard_map/ppermute | solution.py:28
  2.5 0.4 %second_states.1 = (f32[4,128,128]{2,1,0:T(8,128)S(1)}, f32[4,128,128]{2,1,0:T(8,128)S(1)}, f32[4,128,128]{2,1,0:T(8,128)S(1)}) custom-call(bf16[128,1024]{1,0:T(8,128)(2,1)S(1)} %get-tuple-element.32.q_ref, bf16[128,1024]{1,0:T(8,128)(2,1)S(1)} %get-tuple-element.29.k_ref.refs_0_, bf16[128,1024]{1,0:T(8,128)(2,1)S(1)} %get-tuple-element.30.v_ref.refs_1_, ...), custom_call_target="tpu_custom_call" | custom-call | tf_op jit(solution)/shard_map/second_states/pallas_call | solution.py:44
  2.8 0.1 collective-permute-start.4
  3.0 0.7 %collective-permute-done.refs_10_ = f32[4,128,128]{2,1,0:T(8,128)S(1)} collective-permute-done((f32[4,128,128]{2,1,0:T(8,128)S(1)}, f32[4,128,128]{2,1,0:T(8,128)S(1)}, u32[]{:S(2)}, u32[]{:S(2)}) %collective-permute-start) | collective-permute-done | bytes 262176 | tf_op jit(solution)/shard_map/ppermute | solution.py:28
  3.6 4.0 %collective-permute-start.3 = (f32[128,128]{1,0:T(8,128)S(1)}, f32[128,128]{1,0:T(8,128)S(1)}, u32[]{:S(2)}, u32[]{:S(2)}) collective-permute-start(f32[128,128]{1,0:T(8,128)S(1)} %get-tuple-element.61), channel_id=1, source_target_pairs={{0,6},{1,7},{2,4},{3,5},{4,2},{5,3},{6,0},{7,1},{8,14},{9,15},{10,... | collective-permute-start | bytes 196616 | tf_op jit(solution)/shard_map/ppermute | solution.py:28
  7.6 0.4 %collective-permute-start.2 = (f32[128,128]{1,0:T(8,128)S(1)}, f32[128,128]{1,0:T(8,128)S(1)}, u32[]{:S(2)}, u32[]{:S(2)}) collective-permute-start(f32[128,128]{1,0:T(8,128)S(1)} %get-tuple-element.62), channel_id=1, source_target_pairs={{0,4},{1,5},{2,6},{3,7},{4,0},{5,1},{6,2},{7,3},{8,12},{9,13},{10,... | collective-permute-start | bytes 196616 | tf_op jit(solution)/shard_map/ppermute | solution.py:28
  8.1 0.2 collective-permute-start.1
  8.3 0.0 collective-permute-done.4.refs_11_
  8.3 2.9 %collective-permute-start.7 = (f32[128,128]{1,0:T(8,128)S(1)}, f32[128,128]{1,0:T(8,128)S(1)}, u32[]{:S(2)}, u32[]{:S(2)}) collective-permute-start(f32[128,128]{1,0:T(8,128)S(1)} %get-tuple-element.57), channel_id=1, source_target_pairs={{0,6},{1,7},{2,4},{3,5},{4,2},{5,3},{6,0},{7,1},{8,14},{9,15},{10,... | collective-permute-start | bytes 196616 | tf_op jit(solution)/shard_map/ppermute | solution.py:28
  11.2 0.4 %collective-permute-start.6 = (f32[128,128]{1,0:T(8,128)S(1)}, f32[128,128]{1,0:T(8,128)S(1)}, u32[]{:S(2)}, u32[]{:S(2)}) collective-permute-start(f32[128,128]{1,0:T(8,128)S(1)} %get-tuple-element.58), channel_id=1, source_target_pairs={{0,4},{1,5},{2,6},{3,7},{4,0},{5,1},{6,2},{7,3},{8,12},{9,13},{10,... | collective-permute-start | bytes 196616 | tf_op jit(solution)/shard_map/ppermute | solution.py:28
  11.7 0.6 %collective-permute-done.2.refs_2_ = f32[128,128]{1,0:T(8,128)S(1)} collective-permute-done((f32[128,128]{1,0:T(8,128)S(1)}, f32[128,128]{1,0:T(8,128)S(1)}, u32[]{:S(2)}, u32[]{:S(2)}) %collective-permute-start.2) | collective-permute-done | bytes 65568 | tf_op jit(solution)/shard_map/ppermute | solution.py:28
  12.2 0.5 %collective-permute-start.5 = (f32[128,128]{1,0:T(8,128)S(1)}, f32[128,128]{1,0:T(8,128)S(1)}, u32[]{:S(2)}, u32[]{:S(2)}) collective-permute-start(f32[128,128]{1,0:T(8,128)S(1)} %get-tuple-element.59), channel_id=1, source_target_pairs={{0,2},{1,3},{2,0},{3,1},{4,6},{5,7},{6,4},{7,5},{8,10},{9,11},{10,... | collective-permute-start | bytes 196616 | tf_op jit(solution)/shard_map/ppermute | solution.py:28
  12.8 0.2 collective-permute-done.1.refs_1_
  13.0 2.6 %collective-permute-start.8 = (f32[128,128]{1,0:T(8,128)S(1)}, f32[128,128]{1,0:T(8,128)S(1)}, u32[]{:S(2)}, u32[]{:S(2)}) collective-permute-start(f32[128,128]{1,0:T(8,128)S(1)} %add.73), channel_id=1, source_target_pairs={{0,8},{1,9},{2,10},{3,11},{4,12},{5,13},{6,14},{7,15},{8,0},{9,1},... | collective-permute-start | bytes 196616 | tf_op jit(solution)/shard_map/ppermute | solution.py:28
  15.6 0.1 scan_a.1
  15.7 0.5 %collective-permute-done.6.refs_6_ = f32[128,128]{1,0:T(8,128)S(1)} collective-permute-done((f32[128,128]{1,0:T(8,128)S(1)}, f32[128,128]{1,0:T(8,128)S(1)}, u32[]{:S(2)}, u32[]{:S(2)}) %collective-permute-start.6) | collective-permute-done | bytes 65568 | tf_op jit(solution)/shard_map/ppermute | solution.py:28
  16.2 0.3 %collective-permute-done.5.refs_5_ = f32[128,128]{1,0:T(8,128)S(1)} collective-permute-done((f32[128,128]{1,0:T(8,128)S(1)}, f32[128,128]{1,0:T(8,128)S(1)}, u32[]{:S(2)}, u32[]{:S(2)}) %collective-permute-start.5) | collective-permute-done | bytes 65568 | tf_op jit(solution)/shard_map/ppermute | solution.py:28
  16.5 1.8 %collective-permute-done.8.refs_8_ = f32[128,128]{1,0:T(8,128)S(1)} collective-permute-done((f32[128,128]{1,0:T(8,128)S(1)}, f32[128,128]{1,0:T(8,128)S(1)}, u32[]{:S(2)}, u32[]{:S(2)}) %collective-permute-start.8) | collective-permute-done | bytes 65568 | tf_op jit(solution)/shard_map/ppermute | solution.py:28
  18.3 0.1 scan_b.1
  18.4 1.9 %collective-permute-start.10 = (f32[2,128,128]{2,1,0:T(8,128)S(1)}, f32[2,128,128]{2,1,0:T(8,128)S(1)}, u32[]{:S(2)}, u32[]{:S(2)}) collective-permute-start(f32[2,128,128]{2,1,0:T(8,128)S(1)} %get-tuple-element.49), channel_id=1, source_target_pairs={{0,6},{1,7},{2,4},{3,5},{4,2},{5,3},{6,0},{7,1},{8,14},{9,15},{10,... | collective-permute-start | bytes 393224 | tf_op jit(solution)/shard_map/ppermute | solution.py:28
  20.2 1.1 %collective-permute-start.9 = (f32[2,128,128]{2,1,0:T(8,128)S(1)}, f32[2,128,128]{2,1,0:T(8,128)S(1)}, u32[]{:S(2)}, u32[]{:S(2)}) collective-permute-start(f32[2,128,128]{2,1,0:T(8,128)S(1)} %get-tuple-element.41), channel_id=1, source_target_pairs={{0,2},{1,3},{2,0},{3,1},{4,6},{5,7},{6,4},{7,5},{8,10},{9,11},{10,... | collective-permute-start | bytes 393224 | tf_op jit(solution)/shard_map/ppermute | solution.py:28
  21.3 0.6 %collective-permute-start.12 = (f32[2,128,128]{2,1,0:T(8,128)S(1)}, f32[2,128,128]{2,1,0:T(8,128)S(1)}, u32[]{:S(2)}, u32[]{:S(2)}) collective-permute-start(f32[2,128,128]{2,1,0:T(8,128)S(1)} %get-tuple-element.51), channel_id=1, source_target_pairs={{0,4},{1,5},{2,6},{3,7},{4,0},{5,1},{6,2},{7,3},{8,12},{9,13},{10,... | collective-permute-start | bytes 393224 | tf_op jit(solution)/shard_map/ppermute | solution.py:28
  22.0 1.9 %inner.1 = (f32[128,1024]{1,0:T(8,128)S(1)}, f32[128,1024]{1,0:T(8,128)S(1)}, f32[128,1024]{1,0:T(8,128)S(1)}) custom-call(bf16[128,1024]{1,0:T(8,128)(2,1)S(1)} %get-tuple-element.32.q_ref, bf16[128,1024]{1,0:T(8,128)(2,1)S(1)} %get-tuple-element.29.k_ref.refs_0_, bf16[128,1024]{1,0:T(8,128)(2,1)S(1)} %get-tuple-element.30.v_ref.refs_1_, ...), custom_call_target="tpu_custom_call" | custom-call | tf_op jit(solution)/shard_map/inner/pallas_call | solution.py:44
  23.9 1.2 %collective-permute-done.10.refs_3_.refs_9_ = f32[2,128,128]{2,1,0:T(8,128)S(1)} collective-permute-done((f32[2,128,128]{2,1,0:T(8,128)S(1)}, f32[2,128,128]{2,1,0:T(8,128)S(1)}, u32[]{:S(2)}, u32[]{:S(2)}) %collective-permute-start.10) | collective-permute-done | bytes 131104 | tf_op jit(solution)/shard_map/ppermute | solution.py:28
  25.1 0.1 collective-permute-start.11
  25.1 1.0 %collective-permute-done.9.refs_2_.refs_7_ = f32[2,128,128]{2,1,0:T(8,128)S(1)} collective-permute-done((f32[2,128,128]{2,1,0:T(8,128)S(1)}, f32[2,128,128]{2,1,0:T(8,128)S(1)}, u32[]{:S(2)}, u32[]{:S(2)}) %collective-permute-start.9) | collective-permute-done | bytes 131104 | tf_op jit(solution)/shard_map/ppermute | solution.py:28
  26.1 0.2 collective-permute-done.12.refs_3_.refs_8_
  26.4 0.1 collective-permute-start.13
  26.5 1.1 %final.2 = (bf16[128,1024]{1,0:T(8,128)(2,1)}, bf16[128,1024]{1,0:T(8,128)(2,1)}, bf16[128,1024]{1,0:T(8,128)(2,1)}) custom-call(bf16[128,1024]{1,0:T(8,128)(2,1)S(1)} %get-tuple-element.29.k_ref.refs_0_, bf16[128,1024]{1,0:T(8,128)(2,1)S(1)} %get-tuple-element.30.v_ref.refs_1_, bf16[128,1024]{1,0:T(8,128)(2,1)S(1)} %get-tuple-element.31.g_ref.refs_2_, ...), custom_call_target="tpu_custom_call" | custom-call | tf_op jit(solution)/shard_map/final/pallas_call | solution.py:184
  27.6 0.4 %collective-permute-done.13.refs_7_ = f32[2,2,128,128]{3,2,1,0:T(8,128)S(1)} collective-permute-done((f32[2,2,128,128]{3,2,1,0:T(8,128)S(1)}, f32[2,2,128,128]{3,2,1,0:T(8,128)S(1)}, u32[]{:S(2)}, u32[]{:S(2)}) %collective-permute-start.13) | collective-permute-done | bytes 262176 | tf_op jit(solution)/shard_map/ppermute | solution.py:28
  28.0 1.1 %final.3 = (bf16[128,1024]{1,0:T(8,128)(2,1)}, bf16[128,1024]{1,0:T(8,128)(2,1)}, bf16[128,1024]{1,0:T(8,128)(2,1)}) custom-call(bf16[128,1024]{1,0:T(8,128)(2,1)S(1)} %get-tuple-element.29.k_ref.refs_0_, bf16[128,1024]{1,0:T(8,128)(2,1)S(1)} %get-tuple-element.30.v_ref.refs_1_, ...), custom_call_target="tpu_custom_call", output_to_operand_aliasing={{0}: (8, {}), {1}: (9, {}), {2}: (10, {})} | custom-call | tf_op jit(solution)/shard_map/final/pallas_call | solution.py:184
  (10 shorter events, 0.2 us)
Async XLA Ops:
  1.9 1.7 %collective-permute-start = (f32[4,128,128]{2,1,0:T(8,128)S(1)}, f32[4,128,128]{2,1,0:T(8,128)S(1)}, u32[]{:S(2)}, u32[]{:S(2)}) collective-permute-start(f32[4,128,128]{2,1,0:T(8,128)S(1)} %get-tuple-element.34), channel_id=1, source_target_pairs={{0,1},{1,0},{2,3},{3,2},{4,5},{5,4},{6,7},{7,6},{8,9},{9,8},{10,11... | collective-permute-start | bytes 786440 | tf_op jit(solution)/shard_map/ppermute | solution.py:28
  2.8 5.4 %collective-permute-start.4 = (f32[4,128,128]{2,1,0:T(8,128)S(1)}, f32[4,128,128]{2,1,0:T(8,128)S(1)}, u32[]{:S(2)}, u32[]{:S(2)}) collective-permute-start(f32[4,128,128]{2,1,0:T(8,128)S(1)} %get-tuple-element.40), channel_id=1, source_target_pairs={{0,1},{1,0},{2,3},{3,2},{4,5},{5,4},{6,7},{7,6},{8,9},{9,8},{10,11... | collective-permute-start | bytes 786440 | tf_op jit(solution)/shard_map/ppermute | solution.py:28
  3.6 9.2 %collective-permute-start.3 = (f32[128,128]{1,0:T(8,128)S(1)}, f32[128,128]{1,0:T(8,128)S(1)}, u32[]{:S(2)}, u32[]{:S(2)}) collective-permute-start(f32[128,128]{1,0:T(8,128)S(1)} %get-tuple-element.61), channel_id=1, source_target_pairs={{0,6},{1,7},{2,4},{3,5},{4,2},{5,3},{6,0},{7,1},{8,14},{9,15},{10,... | collective-permute-start | bytes 196616 | tf_op jit(solution)/shard_map/ppermute | solution.py:28
  7.6 4.6 %collective-permute-start.2 = (f32[128,128]{1,0:T(8,128)S(1)}, f32[128,128]{1,0:T(8,128)S(1)}, u32[]{:S(2)}, u32[]{:S(2)}) collective-permute-start(f32[128,128]{1,0:T(8,128)S(1)} %get-tuple-element.62), channel_id=1, source_target_pairs={{0,4},{1,5},{2,6},{3,7},{4,0},{5,1},{6,2},{7,3},{8,12},{9,13},{10,... | collective-permute-start | bytes 196616 | tf_op jit(solution)/shard_map/ppermute | solution.py:28
  8.1 5.0 %collective-permute-start.1 = (f32[128,128]{1,0:T(8,128)S(1)}, f32[128,128]{1,0:T(8,128)S(1)}, u32[]{:S(2)}, u32[]{:S(2)}) collective-permute-start(f32[128,128]{1,0:T(8,128)S(1)} %get-tuple-element.63), channel_id=1, source_target_pairs={{0,2},{1,3},{2,0},{3,1},{4,6},{5,7},{6,4},{7,5},{8,10},{9,11},{10,... | collective-permute-start | bytes 196616 | tf_op jit(solution)/shard_map/ppermute | solution.py:28
  8.3 7.4 %collective-permute-start.7 = (f32[128,128]{1,0:T(8,128)S(1)}, f32[128,128]{1,0:T(8,128)S(1)}, u32[]{:S(2)}, u32[]{:S(2)}) collective-permute-start(f32[128,128]{1,0:T(8,128)S(1)} %get-tuple-element.57), channel_id=1, source_target_pairs={{0,6},{1,7},{2,4},{3,5},{4,2},{5,3},{6,0},{7,1},{8,14},{9,15},{10,... | collective-permute-start | bytes 196616 | tf_op jit(solution)/shard_map/ppermute | solution.py:28
  11.2 5.0 %collective-permute-start.6 = (f32[128,128]{1,0:T(8,128)S(1)}, f32[128,128]{1,0:T(8,128)S(1)}, u32[]{:S(2)}, u32[]{:S(2)}) collective-permute-start(f32[128,128]{1,0:T(8,128)S(1)} %get-tuple-element.58), channel_id=1, source_target_pairs={{0,4},{1,5},{2,6},{3,7},{4,0},{5,1},{6,2},{7,3},{8,12},{9,13},{10,... | collective-permute-start | bytes 196616 | tf_op jit(solution)/shard_map/ppermute | solution.py:28
  12.2 4.3 %collective-permute-start.5 = (f32[128,128]{1,0:T(8,128)S(1)}, f32[128,128]{1,0:T(8,128)S(1)}, u32[]{:S(2)}, u32[]{:S(2)}) collective-permute-start(f32[128,128]{1,0:T(8,128)S(1)} %get-tuple-element.59), channel_id=1, source_target_pairs={{0,2},{1,3},{2,0},{3,1},{4,6},{5,7},{6,4},{7,5},{8,10},{9,11},{10,... | collective-permute-start | bytes 196616 | tf_op jit(solution)/shard_map/ppermute | solution.py:28
  13.0 5.2 %collective-permute-start.8 = (f32[128,128]{1,0:T(8,128)S(1)}, f32[128,128]{1,0:T(8,128)S(1)}, u32[]{:S(2)}, u32[]{:S(2)}) collective-permute-start(f32[128,128]{1,0:T(8,128)S(1)} %add.73), channel_id=1, source_target_pairs={{0,8},{1,9},{2,10},{3,11},{4,12},{5,13},{6,14},{7,15},{8,0},{9,1},... | collective-permute-start | bytes 196616 | tf_op jit(solution)/shard_map/ppermute | solution.py:28
  18.4 6.7 %collective-permute-start.10 = (f32[2,128,128]{2,1,0:T(8,128)S(1)}, f32[2,128,128]{2,1,0:T(8,128)S(1)}, u32[]{:S(2)}, u32[]{:S(2)}) collective-permute-start(f32[2,128,128]{2,1,0:T(8,128)S(1)} %get-tuple-element.49), channel_id=1, source_target_pairs={{0,6},{1,7},{2,4},{3,5},{4,2},{5,3},{6,0},{7,1},{8,14},{9,15},{10,... | collective-permute-start | bytes 393224 | tf_op jit(solution)/shard_map/ppermute | solution.py:28
  20.2 5.9 %collective-permute-start.9 = (f32[2,128,128]{2,1,0:T(8,128)S(1)}, f32[2,128,128]{2,1,0:T(8,128)S(1)}, u32[]{:S(2)}, u32[]{:S(2)}) collective-permute-start(f32[2,128,128]{2,1,0:T(8,128)S(1)} %get-tuple-element.41), channel_id=1, source_target_pairs={{0,2},{1,3},{2,0},{3,1},{4,6},{5,7},{6,4},{7,5},{8,10},{9,11},{10,... | collective-permute-start | bytes 393224 | tf_op jit(solution)/shard_map/ppermute | solution.py:28
  21.3 5.0 %collective-permute-start.12 = (f32[2,128,128]{2,1,0:T(8,128)S(1)}, f32[2,128,128]{2,1,0:T(8,128)S(1)}, u32[]{:S(2)}, u32[]{:S(2)}) collective-permute-start(f32[2,128,128]{2,1,0:T(8,128)S(1)} %get-tuple-element.51), channel_id=1, source_target_pairs={{0,4},{1,5},{2,6},{3,7},{4,0},{5,1},{6,2},{7,3},{8,12},{9,13},{10,... | collective-permute-start | bytes 393224 | tf_op jit(solution)/shard_map/ppermute | solution.py:28
  25.1 2.5 %collective-permute-start.11 = (f32[2,2,128,128]{3,2,1,0:T(8,128)S(1)}, f32[2,2,128,128]{3,2,1,0:T(8,128)S(1)}, u32[]{:S(2)}, u32[]{:S(2)}) collective-permute-start(f32[2,2,128,128]{3,2,1,0:T(8,128)S(1)} %pair.2), channel_id=1, source_target_pairs={{0,1},{1,0},{2,3},{3,2},{4,5},{5,4},{6,7},{7,6},{8,9},{9,8},{10,11... | collective-permute-start | bytes 786440 | tf_op jit(solution)/shard_map/ppermute | solution.py:28
  26.4 1.6 %collective-permute-start.13 = (f32[2,2,128,128]{3,2,1,0:T(8,128)S(1)}, f32[2,2,128,128]{3,2,1,0:T(8,128)S(1)}, u32[]{:S(2)}, u32[]{:S(2)}) collective-permute-start(f32[2,2,128,128]{3,2,1,0:T(8,128)S(1)} %pair.3), channel_id=1, source_target_pairs={{0,1},{1,0},{2,3},{3,2},{4,5},{5,4},{6,7},{7,6},{8,9},{9,8},{10,11... | collective-permute-start | bytes 786440 | tf_op jit(solution)/shard_map/ppermute | solution.py:28

commit v4 on v3

--- a/solution.py
+++ b/solution.py
@@ -125,6 +125,10 @@
     return total
 
 
+def sum_kernel(*refs):
+    refs[4][...] = (refs[0][...] + refs[1][...]) + (refs[2][...] + refs[3][...])
+
+
 def scan_a_kernel(*refs):
     parts, ahead, outs = refs[:4], refs[4:-4], refs[-4:]
     _, chip, _, even = place()
@@ -134,7 +138,8 @@
 
 
 def scan_b_kernel(*refs):
-    scanned_a, parts, ahead, outs = refs[:4], refs[4:8], refs[8], refs[9:]
+    scanned_a, ahead, outs = refs[:4], refs[8], refs[9:]
+    parts = [refs[4 + n] for n in (0, 1, 2, 3)]
     _, chip, _, even = place()
     for slot in range(4):
         outs[slot][0] = scanned_a[slot][...]
@@ -150,43 +155,46 @@
         out[n, 1] = refs[n][1] + jnp.where(last, keep_b[slot], 0.0)
 
 
-def final_kernel(factor, half, k_ref, v_ref, g_ref, qi_ref, ki_ref, vi_ref, *refs):
+def final_kernel(factor, work, k_ref, v_ref, g_ref, qi_ref, ki_ref, vi_ref, *refs):
     qo_hbm, ko_hbm, vo_hbm, buffer, sems = refs[-5:]
     core, chip, _, even = place()
     last = (core == 1) == even
 
-    def total(slot, i):
+    def total(half, slot, i):
         if half == 1:
-            for ref, slots in zip(refs, PIECES):
-                if slot in slots:
-                    return ref[slots.index(slot), i].astype(jnp.bfloat16)
+            piece = [slot in slots for slots in PIECES].index(True)
+            ref = refs[6] if piece == 0 else refs[0]
+            return ref[PIECES[piece].index(slot), i].astype(jnp.bfloat16)
         use = last if i == 0 else jnp.logical_not(last)
         return (refs[slot][i] + jnp.where(use, refs[4 + i][slot], 0.0)).astype(jnp.bfloat16)
 
     stores = []
-    for slot in (slot for slots in PIECES for slot in slots):
+    for n, (half, slot) in enumerate(work):
         cols = columns(half, slot, core, chip)
-        a, b = total(slot, 0), total(slot, 1)
+        a, b = total(half, slot, 0), total(half, slot, 1)
         earlier, future = jnp.where(even, a, b), jnp.where(even, b, a)
         qo = qi_ref[:, cols] + dot(g_ref[:, cols], earlier, ((1,), (1,)))
         ko = ki_ref[:, cols] + dot(v_ref[:, cols], future, ((1,), (1,)))
         vo = vi_ref[:, cols] + dot(k_ref[:, cols], future, ((1,), (0,)))
         for i, (value, out) in enumerate(((qo, qo_hbm), (ko, ko_hbm), (vo, vo_hbm))):
-            buffer[i, slot] = (factor * value).astype(jnp.bfloat16)
-            stores.append(pltpu.make_async_copy(buffer.at[i, slot], out.at[:, cols], sems.at[i, slot]))
+            buffer[i, n] = (factor * value).astype(jnp.bfloat16)
+            stores.append(pltpu.make_async_copy(buffer.at[i, n], out.at[:, cols], sems.at[i, n]))
             stores[-1].start()
     for store in stores:
         store.wait()
 
 
-def final(factor, half, inputs, outs=()):
+def final(factor, work, inputs, outs=()):
     out = jax.ShapeDtypeStruct(inputs[0].shape, jnp.bfloat16)
     return pl.pallas_call(
-        lambda *refs: final_kernel(factor, half, *refs),
+        lambda *refs: final_kernel(factor, work, *refs),
         out_shape=(out, out, out),
         in_specs=[VMEM] * len(inputs) + [HBM] * len(outs),
         out_specs=(HBM,) * 3,
-        scratch_shapes=[pltpu.VMEM((3, 4, GROUP, HEAD_DIM), jnp.bfloat16), pltpu.SemaphoreType.DMA((3, 4))],
+        scratch_shapes=[
+            pltpu.VMEM((3, len(work), GROUP, HEAD_DIM), jnp.bfloat16),
+            pltpu.SemaphoreType.DMA((3, len(work))),
+        ],
         input_output_aliases={len(inputs) + i: i for i in range(len(outs))},
         compiler_params=PARAMS,
         name="final",
@@ -219,6 +227,7 @@
 
 def local(*args):
     devices = lax.axis_size(AXIS)
+    assert args[0].shape[0] == GROUP and devices % 8 == 0
     factor = 1.0 / math.sqrt(HEAD_DIM * args[0].shape[0] * devices)
 
     *args, send_a = first_states(args)
@@ -230,12 +239,10 @@
 
     parts_a = [keep_a[0] + got_a[0]] + [swap(keep_a[m] + got_a[m], 2 * m) for m in (1, 2, 3)]
     parts_b = [keep_b[0] + got_b[0]] + [swap(keep_b[m] + got_b[m], 2 * m) for m in (1, 2, 3)]
-    sum_a = parts_a[0]
-    for m in (2, 3, 1):
-        (sum_a,) = lax.optimization_barrier((sum_a + parts_a[m],))
+    sum_a = in_vmem(sum_kernel, heads(), [parts_a[m] for m in (0, 3, 2, 1)], "sum_a")
     ahead = between_squares(sum_a, sum(parts_b[1:], parts_b[0]), devices // 8)
     scanned = in_vmem(scan_a_kernel, (heads(),) * 4, (*parts_a, *ahead[:-1]), "scan_a")
-    scanned = in_vmem(scan_b_kernel, (heads(2),) * 4, (*scanned, *parts_b, ahead[-1]), "scan_b")
+    scanned = in_vmem(scan_b_kernel, (heads(2),) * 4, (*scanned, *(parts_b[m] for m in (0, 1, 2, 3)), ahead[-1]), "scan_b")
     back = [scanned[0]] + [swap(scanned[m], 2 * m) for m in (1, 2, 3)]
     back[1], own_part = lax.optimization_barrier((back[1], own_part))
 
@@ -245,8 +252,9 @@
         pair = in_vmem(kernel, heads(len(slots), 2), (keep_a, keep_b, *(back[m] for m in slots)), "pair")
         others.append(swap(pair, 1))
     inputs = (*args[1:], *own_part)
-    outs = final(factor, 0, (*inputs, *back, got_a, got_b))
-    return final(factor, 1, (*inputs, *others), outs)
+    work = [(0, slot) for slots in PIECES for slot in slots] + [(1, slot) for slot in PIECES[0]]
+    outs = final(factor, work, (*inputs, *back, got_a, got_b, others[0]))
+    return final(factor, [(1, slot) for slot in PIECES[1]], (*inputs, others[1]), outs)
 
 
 def solution(mesh):

time: 29.2 us -> 29 us (level)
    pallas_call x6 -> x7, Pallas kernels: 2.46 us -> 2.47 us  [in_vmem(): pl.pallas_call(kernel, out_shape=out_shape, in_specs=[VMEM] * len(args),...]
  transfers between devices with their start and end apart: 14 -> 14, of which waited for: 10 -> 10; matrix products, arithmetic and copies ran while one was open for 0% -> 0% of each run, Pallas kernels for 12% -> 13%
where the time goes in v4:
time: 29 us; the launch traced here: 28.9 us
  starting transfers between devices  15.3 us (53%)
  waiting for transfers between devices  6.85 us (24%)
  Pallas kernels  5.96 us (21%)
  between operations  0.72 us (2%)
    ppermute x14, starting transfers between devices, swap(): return lax.ppermute(x, AXIS, [(i, i ^ mask) for i in range(count)])  15.3 us
    ppermute x14, waiting for transfers between devices, swap(): return lax.ppermute(x, AXIS, [(i, i ^ mask) for i in range(count)])  6.85 us
    pallas_call x7, Pallas kernels, in_vmem(): pl.pallas_call(kernel, out_shape=out_shape, in_specs=[VMEM] * len(args),...  2.47 us
    pallas_call x2, Pallas kernels, final(): pl.pallas_call(lambda *refs: final_kernel(factor, work, *refs), out_shape...  2.19 us
    pallas_call x1, Pallas kernels, first_states(): pl.pallas_call(first_kernel, out_shape=(rows,) * 4 + (heads(4),), in_spec...  1.3 us
  transfers between devices with their start and end apart: 14, of which 10 were waited for; matrix products, arithmetic and copies ran while one was open for 0% of the time, Pallas kernels for 13%

profile of v4, /device:TPU:0, one launch (start us, length us, event | category | flops | bytes accessed | tf_op | source)
XLA Modules:
  0.0 28.9 jit_solution(8033066496738307053)
XLA Ops:
  0.6 1.3 %first_states.1 = (bf16[128,1024]{1,0:T(8,128)(2,1)S(1)}, bf16[128,1024]{1,0:T(8,128)(2,1)S(1)}, bf16[128,1024]{1,0:T(8,128)(2,1)S(1)}, bf16[128,1024]{1,0:T(8,128)(2,1)S(1)}, f32[4,128,128]{2,1,0:T(8,128)S(1)}) custom-call(bf16[128,1024]{1,0:T(8,128)(2,1)} %q_hbm.1, bf16[128,1024]{1,0:T(8,128)(2,1)} %k_hbm.1, bf16[128,1024]{1,0:T(8,128)(2,1)} %v_hbm.1, ...), custom_call_target="tpu_custom_call" | custom-call | tf_op jit(solution)/shard_map/first_states/pallas_call | solution.py:82
  1.9 0.5 %collective-permute-start = (f32[4,128,128]{2,1,0:T(8,128)S(1)}, f32[4,128,128]{2,1,0:T(8,128)S(1)}, u32[]{:S(2)}, u32[]{:S(2)}) collective-permute-start(f32[4,128,128]{2,1,0:T(8,128)S(1)} %get-tuple-element.34), channel_id=1, source_target_pairs={{0,1},{1,0},{2,3},{3,2},{4,5},{5,4},{6,7},{7,6},{8,9},{9,8},{10,11... | collective-permute-start | bytes 786440 | tf_op jit(solution)/shard_map/ppermute | solution.py:28
  2.5 0.4 %second_states.1 = (f32[4,128,128]{2,1,0:T(8,128)S(1)}, f32[4,128,128]{2,1,0:T(8,128)S(1)}, f32[4,128,128]{2,1,0:T(8,128)S(1)}) custom-call(bf16[128,1024]{1,0:T(8,128)(2,1)S(1)} %get-tuple-element.32.q_ref, bf16[128,1024]{1,0:T(8,128)(2,1)S(1)} %get-tuple-element.29.k_ref.refs_0_, bf16[128,1024]{1,0:T(8,128)(2,1)S(1)} %get-tuple-element.30.v_ref.refs_1_, ...), custom_call_target="tpu_custom_call" | custom-call | tf_op jit(solution)/shard_map/second_states/pallas_call | solution.py:44
  2.8 0.1 collective-permute-start.4
  3.0 0.7 %collective-permute-done.refs_10_ = f32[4,128,128]{2,1,0:T(8,128)S(1)} collective-permute-done((f32[4,128,128]{2,1,0:T(8,128)S(1)}, f32[4,128,128]{2,1,0:T(8,128)S(1)}, u32[]{:S(2)}, u32[]{:S(2)}) %collective-permute-start) | collective-permute-done | bytes 262176 | tf_op jit(solution)/shard_map/ppermute | solution.py:28
  3.7 4.0 %collective-permute-start.3 = (f32[128,128]{1,0:T(8,128)S(1)}, f32[128,128]{1,0:T(8,128)S(1)}, u32[]{:S(2)}, u32[]{:S(2)}) collective-permute-start(f32[128,128]{1,0:T(8,128)S(1)} %get-tuple-element.59), channel_id=1, source_target_pairs={{0,6},{1,7},{2,4},{3,5},{4,2},{5,3},{6,0},{7,1},{8,14},{9,15},{10,... | collective-permute-start | bytes 196616 | tf_op jit(solution)/shard_map/ppermute | solution.py:28
  7.6 0.4 %collective-permute-start.2 = (f32[128,128]{1,0:T(8,128)S(1)}, f32[128,128]{1,0:T(8,128)S(1)}, u32[]{:S(2)}, u32[]{:S(2)}) collective-permute-start(f32[128,128]{1,0:T(8,128)S(1)} %get-tuple-element.60), channel_id=1, source_target_pairs={{0,4},{1,5},{2,6},{3,7},{4,0},{5,1},{6,2},{7,3},{8,12},{9,13},{10,... | collective-permute-start | bytes 196616 | tf_op jit(solution)/shard_map/ppermute | solution.py:28
  8.1 0.2 collective-permute-start.1
  8.3 0.0 collective-permute-done.4.refs_11_
  8.3 2.9 %collective-permute-start.7 = (f32[128,128]{1,0:T(8,128)S(1)}, f32[128,128]{1,0:T(8,128)S(1)}, u32[]{:S(2)}, u32[]{:S(2)}) collective-permute-start(f32[128,128]{1,0:T(8,128)S(1)} %get-tuple-element.55), channel_id=1, source_target_pairs={{0,6},{1,7},{2,4},{3,5},{4,2},{5,3},{6,0},{7,1},{8,14},{9,15},{10,... | collective-permute-start | bytes 196616 | tf_op jit(solution)/shard_map/ppermute | solution.py:28
  11.2 0.4 %collective-permute-start.6 = (f32[128,128]{1,0:T(8,128)S(1)}, f32[128,128]{1,0:T(8,128)S(1)}, u32[]{:S(2)}, u32[]{:S(2)}) collective-permute-start(f32[128,128]{1,0:T(8,128)S(1)} %get-tuple-element.56), channel_id=1, source_target_pairs={{0,4},{1,5},{2,6},{3,7},{4,0},{5,1},{6,2},{7,3},{8,12},{9,13},{10,... | collective-permute-start | bytes 196616 | tf_op jit(solution)/shard_map/ppermute | solution.py:28
  11.7 0.4 %collective-permute-start.5 = (f32[128,128]{1,0:T(8,128)S(1)}, f32[128,128]{1,0:T(8,128)S(1)}, u32[]{:S(2)}, u32[]{:S(2)}) collective-permute-start(f32[128,128]{1,0:T(8,128)S(1)} %get-tuple-element.57), channel_id=1, source_target_pairs={{0,2},{1,3},{2,0},{3,1},{4,6},{5,7},{6,4},{7,5},{8,10},{9,11},{10,... | collective-permute-start | bytes 196616 | tf_op jit(solution)/shard_map/ppermute | solution.py:28
  12.1 0.2 collective-permute-done.2.refs_2_
  12.2 0.8 %collective-permute-done.1.refs_1_.refs_3_ = f32[128,128]{1,0:T(8,128)S(1)} collective-permute-done((f32[128,128]{1,0:T(8,128)S(1)}, f32[128,128]{1,0:T(8,128)S(1)}, u32[]{:S(2)}, u32[]{:S(2)}) %collective-permute-start.1) | collective-permute-done | bytes 65568 | tf_op jit(solution)/shard_map/ppermute | solution.py:28
  13.1 2.6 %collective-permute-start.8 = (f32[128,128]{1,0:T(8,128)S(1)}, f32[128,128]{1,0:T(8,128)S(1)}, u32[]{:S(2)}, u32[]{:S(2)}) collective-permute-start(f32[128,128]{1,0:T(8,128)S(1)} %sum_a.1), channel_id=1, source_target_pairs={{0,8},{1,9},{2,10},{3,11},{4,12},{5,13},{6,14},{7,15},{8,0},{9,1},... | collective-permute-start | bytes 196616 | tf_op jit(solution)/shard_map/ppermute | solution.py:28
  15.6 0.1 scan_a.1
  15.7 0.2 collective-permute-done.6.refs_6_
  15.9 0.1 collective-permute-done.5.refs_5_
  15.9 2.4 %collective-permute-done.8.refs_8_ = f32[128,128]{1,0:T(8,128)S(1)} collective-permute-done((f32[128,128]{1,0:T(8,128)S(1)}, f32[128,128]{1,0:T(8,128)S(1)}, u32[]{:S(2)}, u32[]{:S(2)}) %collective-permute-start.8) | collective-permute-done | bytes 65568 | tf_op jit(solution)/shard_map/ppermute | solution.py:28
  18.3 0.1 scan_b.1
  18.4 1.7 %collective-permute-start.12 = (f32[2,128,128]{2,1,0:T(8,128)S(1)}, f32[2,128,128]{2,1,0:T(8,128)S(1)}, u32[]{:S(2)}, u32[]{:S(2)}) collective-permute-start(f32[2,128,128]{2,1,0:T(8,128)S(1)} %get-tuple-element.51), channel_id=1, source_target_pairs={{0,6},{1,7},{2,4},{3,5},{4,2},{5,3},{6,0},{7,1},{8,14},{9,15},{10,... | collective-permute-start | bytes 393224 | tf_op jit(solution)/shard_map/ppermute | solution.py:28
  20.1 1.3 %collective-permute-start.9 = (f32[2,128,128]{2,1,0:T(8,128)S(1)}, f32[2,128,128]{2,1,0:T(8,128)S(1)}, u32[]{:S(2)}, u32[]{:S(2)}) collective-permute-start(f32[2,128,128]{2,1,0:T(8,128)S(1)} %get-tuple-element.41), channel_id=1, source_target_pairs={{0,2},{1,3},{2,0},{3,1},{4,6},{5,7},{6,4},{7,5},{8,10},{9,11},{10,... | collective-permute-start | bytes 393224 | tf_op jit(solution)/shard_map/ppermute | solution.py:28
  21.4 0.6 %collective-permute-start.10 = (f32[2,128,128]{2,1,0:T(8,128)S(1)}, f32[2,128,128]{2,1,0:T(8,128)S(1)}, u32[]{:S(2)}, u32[]{:S(2)}) collective-permute-start(f32[2,128,128]{2,1,0:T(8,128)S(1)} %get-tuple-element.49), channel_id=1, source_target_pairs={{0,4},{1,5},{2,6},{3,7},{4,0},{5,1},{6,2},{7,3},{8,12},{9,13},{10,... | collective-permute-start | bytes 393224 | tf_op jit(solution)/shard_map/ppermute | solution.py:28
  21.9 1.9 %inner.1 = (f32[128,1024]{1,0:T(8,128)S(1)}, f32[128,1024]{1,0:T(8,128)S(1)}, f32[128,1024]{1,0:T(8,128)S(1)}) custom-call(bf16[128,1024]{1,0:T(8,128)(2,1)S(1)} %get-tuple-element.32.q_ref, bf16[128,1024]{1,0:T(8,128)(2,1)S(1)} %get-tuple-element.29.k_ref.refs_0_, bf16[128,1024]{1,0:T(8,128)(2,1)S(1)} %get-tuple-element.30.v_ref.refs_1_, ...), custom_call_target="tpu_custom_call" | custom-call | tf_op jit(solution)/shard_map/inner/pallas_call | solution.py:44
  23.8 0.6 %collective-permute-done.12.refs_3_.refs_9_ = f32[2,128,128]{2,1,0:T(8,128)S(1)} collective-permute-done((f32[2,128,128]{2,1,0:T(8,128)S(1)}, f32[2,128,128]{2,1,0:T(8,128)S(1)}, u32[]{:S(2)}, u32[]{:S(2)}) %collective-permute-start.12) | collective-permute-done | bytes 131104 | tf_op jit(solution)/shard_map/ppermute | solution.py:28
  24.4 0.1 collective-permute-start.13
  24.5 1.2 %collective-permute-done.9.refs_2_.refs_7_ = f32[2,128,128]{2,1,0:T(8,128)S(1)} collective-permute-done((f32[2,128,128]{2,1,0:T(8,128)S(1)}, f32[2,128,128]{2,1,0:T(8,128)S(1)}, u32[]{:S(2)}, u32[]{:S(2)}) %collective-permute-start.9) | collective-permute-done | bytes 131104 | tf_op jit(solution)/shard_map/ppermute | solution.py:28
  25.7 0.6 %collective-permute-done.10.refs_3_.refs_8_ = f32[2,128,128]{2,1,0:T(8,128)S(1)} collective-permute-done((f32[2,128,128]{2,1,0:T(8,128)S(1)}, f32[2,128,128]{2,1,0:T(8,128)S(1)}, u32[]{:S(2)}, u32[]{:S(2)}) %collective-permute-start.10) | collective-permute-done | bytes 131104 | tf_op jit(solution)/shard_map/ppermute | solution.py:28
  26.4 0.1 collective-permute-start.11
  26.5 1.3 %final.2 = (bf16[128,1024]{1,0:T(8,128)(2,1)}, bf16[128,1024]{1,0:T(8,128)(2,1)}, bf16[128,1024]{1,0:T(8,128)(2,1)}) custom-call(bf16[128,1024]{1,0:T(8,128)(2,1)S(1)} %get-tuple-element.29.k_ref.refs_0_, bf16[128,1024]{1,0:T(8,128)(2,1)S(1)} %get-tuple-element.30.v_ref.refs_1_, bf16[128,1024]{1,0:T(8,128)(2,1)S(1)} %get-tuple-element.31.g_ref.refs_2_, ...), custom_call_target="tpu_custom_call" | custom-call | tf_op jit(solution)/shard_map/final/pallas_call | solution.py:189
  27.7 0.2 collective-permute-done.11.refs_6_
  28.0 0.9 %final.3 = (bf16[128,1024]{1,0:T(8,128)(2,1)}, bf16[128,1024]{1,0:T(8,128)(2,1)}, bf16[128,1024]{1,0:T(8,128)(2,1)}) custom-call(bf16[128,1024]{1,0:T(8,128)(2,1)S(1)} %get-tuple-element.29.k_ref.refs_0_, bf16[128,1024]{1,0:T(8,128)(2,1)S(1)} %get-tuple-element.30.v_ref.refs_1_, ...), custom_call_target="tpu_custom_call", output_to_operand_aliasing={{0}: (7, {}), {1}: (8, {}), {2}: (9, {})} | custom-call | tf_op jit(solution)/shard_map/final/pallas_call | solution.py:189
  (8 shorter events, 0.2 us)
Async XLA Ops:
  1.9 1.7 %collective-permute-start = (f32[4,128,128]{2,1,0:T(8,128)S(1)}, f32[4,128,128]{2,1,0:T(8,128)S(1)}, u32[]{:S(2)}, u32[]{:S(2)}) collective-permute-start(f32[4,128,128]{2,1,0:T(8,128)S(1)} %get-tuple-element.34), channel_id=1, source_target_pairs={{0,1},{1,0},{2,3},{3,2},{4,5},{5,4},{6,7},{7,6},{8,9},{9,8},{10,11... | collective-permute-start | bytes 786440 | tf_op jit(solution)/shard_map/ppermute | solution.py:28
  2.8 5.4 %collective-permute-start.4 = (f32[4,128,128]{2,1,0:T(8,128)S(1)}, f32[4,128,128]{2,1,0:T(8,128)S(1)}, u32[]{:S(2)}, u32[]{:S(2)}) collective-permute-start(f32[4,128,128]{2,1,0:T(8,128)S(1)} %get-tuple-element.40), channel_id=1, source_target_pairs={{0,1},{1,0},{2,3},{3,2},{4,5},{5,4},{6,7},{7,6},{8,9},{9,8},{10,11... | collective-permute-start | bytes 786440 | tf_op jit(solution)/shard_map/ppermute | solution.py:28
  3.7 8.0 %collective-permute-start.3 = (f32[128,128]{1,0:T(8,128)S(1)}, f32[128,128]{1,0:T(8,128)S(1)}, u32[]{:S(2)}, u32[]{:S(2)}) collective-permute-start(f32[128,128]{1,0:T(8,128)S(1)} %get-tuple-element.59), channel_id=1, source_target_pairs={{0,6},{1,7},{2,4},{3,5},{4,2},{5,3},{6,0},{7,1},{8,14},{9,15},{10,... | collective-permute-start | bytes 196616 | tf_op jit(solution)/shard_map/ppermute | solution.py:28
  7.6 4.6 %collective-permute-start.2 = (f32[128,128]{1,0:T(8,128)S(1)}, f32[128,128]{1,0:T(8,128)S(1)}, u32[]{:S(2)}, u32[]{:S(2)}) collective-permute-start(f32[128,128]{1,0:T(8,128)S(1)} %get-tuple-element.60), channel_id=1, source_target_pairs={{0,4},{1,5},{2,6},{3,7},{4,0},{5,1},{6,2},{7,3},{8,12},{9,13},{10,... | collective-permute-start | bytes 196616 | tf_op jit(solution)/shard_map/ppermute | solution.py:28
  8.1 5.0 %collective-permute-start.1 = (f32[128,128]{1,0:T(8,128)S(1)}, f32[128,128]{1,0:T(8,128)S(1)}, u32[]{:S(2)}, u32[]{:S(2)}) collective-permute-start(f32[128,128]{1,0:T(8,128)S(1)} %get-tuple-element.61), channel_id=1, source_target_pairs={{0,2},{1,3},{2,0},{3,1},{4,6},{5,7},{6,4},{7,5},{8,10},{9,11},{10,... | collective-permute-start | bytes 196616 | tf_op jit(solution)/shard_map/ppermute | solution.py:28
  8.3 7.4 %collective-permute-start.7 = (f32[128,128]{1,0:T(8,128)S(1)}, f32[128,128]{1,0:T(8,128)S(1)}, u32[]{:S(2)}, u32[]{:S(2)}) collective-permute-start(f32[128,128]{1,0:T(8,128)S(1)} %get-tuple-element.55), channel_id=1, source_target_pairs={{0,6},{1,7},{2,4},{3,5},{4,2},{5,3},{6,0},{7,1},{8,14},{9,15},{10,... | collective-permute-start | bytes 196616 | tf_op jit(solution)/shard_map/ppermute | solution.py:28
  11.2 4.7 %collective-permute-start.6 = (f32[128,128]{1,0:T(8,128)S(1)}, f32[128,128]{1,0:T(8,128)S(1)}, u32[]{:S(2)}, u32[]{:S(2)}) collective-permute-start(f32[128,128]{1,0:T(8,128)S(1)} %get-tuple-element.56), channel_id=1, source_target_pairs={{0,4},{1,5},{2,6},{3,7},{4,0},{5,1},{6,2},{7,3},{8,12},{9,13},{10,... | collective-permute-start | bytes 196616 | tf_op jit(solution)/shard_map/ppermute | solution.py:28
  11.7 4.3 %collective-permute-start.5 = (f32[128,128]{1,0:T(8,128)S(1)}, f32[128,128]{1,0:T(8,128)S(1)}, u32[]{:S(2)}, u32[]{:S(2)}) collective-permute-start(f32[128,128]{1,0:T(8,128)S(1)} %get-tuple-element.57), channel_id=1, source_target_pairs={{0,2},{1,3},{2,0},{3,1},{4,6},{5,7},{6,4},{7,5},{8,10},{9,11},{10,... | collective-permute-start | bytes 196616 | tf_op jit(solution)/shard_map/ppermute | solution.py:28
  13.1 5.2 %collective-permute-start.8 = (f32[128,128]{1,0:T(8,128)S(1)}, f32[128,128]{1,0:T(8,128)S(1)}, u32[]{:S(2)}, u32[]{:S(2)}) collective-permute-start(f32[128,128]{1,0:T(8,128)S(1)} %sum_a.1), channel_id=1, source_target_pairs={{0,8},{1,9},{2,10},{3,11},{4,12},{5,13},{6,14},{7,15},{8,0},{9,1},... | collective-permute-start | bytes 196616 | tf_op jit(solution)/shard_map/ppermute | solution.py:28
  18.4 6.0 %collective-permute-start.12 = (f32[2,128,128]{2,1,0:T(8,128)S(1)}, f32[2,128,128]{2,1,0:T(8,128)S(1)}, u32[]{:S(2)}, u32[]{:S(2)}) collective-permute-start(f32[2,128,128]{2,1,0:T(8,128)S(1)} %get-tuple-element.51), channel_id=1, source_target_pairs={{0,6},{1,7},{2,4},{3,5},{4,2},{5,3},{6,0},{7,1},{8,14},{9,15},{10,... | collective-permute-start | bytes 393224 | tf_op jit(solution)/shard_map/ppermute | solution.py:28
  20.1 5.6 %collective-permute-start.9 = (f32[2,128,128]{2,1,0:T(8,128)S(1)}, f32[2,128,128]{2,1,0:T(8,128)S(1)}, u32[]{:S(2)}, u32[]{:S(2)}) collective-permute-start(f32[2,128,128]{2,1,0:T(8,128)S(1)} %get-tuple-element.41), channel_id=1, source_target_pairs={{0,2},{1,3},{2,0},{3,1},{4,6},{5,7},{6,4},{7,5},{8,10},{9,11},{10,... | collective-permute-start | bytes 393224 | tf_op jit(solution)/shard_map/ppermute | solution.py:28
  21.4 5.0 %collective-permute-start.10 = (f32[2,128,128]{2,1,0:T(8,128)S(1)}, f32[2,128,128]{2,1,0:T(8,128)S(1)}, u32[]{:S(2)}, u32[]{:S(2)}) collective-permute-start(f32[2,128,128]{2,1,0:T(8,128)S(1)} %get-tuple-element.49), channel_id=1, source_target_pairs={{0,4},{1,5},{2,6},{3,7},{4,0},{5,1},{6,2},{7,3},{8,12},{9,13},{10,... | collective-permute-start | bytes 393224 | tf_op jit(solution)/shard_map/ppermute | solution.py:28
  24.4 2.0 %collective-permute-start.13 = (f32[2,2,128,128]{3,2,1,0:T(8,128)S(1)}, f32[2,2,128,128]{3,2,1,0:T(8,128)S(1)}, u32[]{:S(2)}, u32[]{:S(2)}) collective-permute-start(f32[2,2,128,128]{3,2,1,0:T(8,128)S(1)} %pair.3), channel_id=1, source_target_pairs={{0,1},{1,0},{2,3},{3,2},{4,5},{5,4},{6,7},{7,6},{8,9},{9,8},{10,11... | collective-permute-start | bytes 786440 | tf_op jit(solution)/shard_map/ppermute | solution.py:28
  26.4 1.6 %collective-permute-start.11 = (f32[2,2,128,128]{3,2,1,0:T(8,128)S(1)}, f32[2,2,128,128]{3,2,1,0:T(8,128)S(1)}, u32[]{:S(2)}, u32[]{:S(2)}) collective-permute-start(f32[2,2,128,128]{3,2,1,0:T(8,128)S(1)} %pair.2), channel_id=1, source_target_pairs={{0,1},{1,0},{2,3},{3,2},{4,5},{5,4},{6,7},{7,6},{8,9},{9,8},{10,11... | collective-permute-start | bytes 786440 | tf_op jit(solution)/shard_map/ppermute | solution.py:28

commit v5 on v4

--- a/solution.py
+++ b/solution.py
@@ -14,7 +14,7 @@
 VMEM = pl.BlockSpec(memory_space=pltpu.VMEM)
 HBM = pl.BlockSpec(memory_space=pltpu.HBM)
 PARAMS = pltpu.CompilerParams(vmem_limit_bytes=16 * 2**20)
-PIECES = ((0, 3), (1, 2))
+PIECES = ((0, 1), (2, 3))
 
 
 def place():
@@ -139,7 +139,7 @@
 
 def scan_b_kernel(*refs):
     scanned_a, ahead, outs = refs[:4], refs[8], refs[9:]
-    parts = [refs[4 + n] for n in (0, 1, 2, 3)]
+    parts = [refs[4 + n] for n in (0, 3, 1, 2)]
     _, chip, _, even = place()
     for slot in range(4):
         outs[slot][0] = scanned_a[slot][...]
@@ -239,12 +239,12 @@
 
     parts_a = [keep_a[0] + got_a[0]] + [swap(keep_a[m] + got_a[m], 2 * m) for m in (1, 2, 3)]
     parts_b = [keep_b[0] + got_b[0]] + [swap(keep_b[m] + got_b[m], 2 * m) for m in (1, 2, 3)]
-    sum_a = in_vmem(sum_kernel, heads(), [parts_a[m] for m in (0, 3, 2, 1)], "sum_a")
+    sum_a = in_vmem(sum_kernel, heads(), [parts_a[m] for m in (0, 2, 3, 1)], "sum_a")
     ahead = between_squares(sum_a, sum(parts_b[1:], parts_b[0]), devices // 8)
     scanned = in_vmem(scan_a_kernel, (heads(),) * 4, (*parts_a, *ahead[:-1]), "scan_a")
-    scanned = in_vmem(scan_b_kernel, (heads(2),) * 4, (*scanned, *(parts_b[m] for m in (0, 1, 2, 3)), ahead[-1]), "scan_b")
+    scanned = in_vmem(scan_b_kernel, (heads(2),) * 4, (*scanned, *(parts_b[m] for m in (0, 2, 3, 1)), ahead[-1]), "scan_b")
     back = [scanned[0]] + [swap(scanned[m], 2 * m) for m in (1, 2, 3)]
-    back[1], own_part = lax.optimization_barrier((back[1], own_part))
+    back[3], own_part = lax.optimization_barrier((back[3], own_part))
 
     others = []
     for slots in PIECES:

time: 29 us -> 28.8 us (level)
  waiting for transfers between devices: 6.85 us -> 6.08 us
  starting transfers between devices: 15.3 us -> 15.8 us
    ppermute x14, waiting for transfers between devices: 6.85 us -> 6.08 us  [swap(): return lax.ppermute(x, AXIS, [(i, i ^ mask) for i in range(count)])]
    ppermute x14, starting transfers between devices: 15.3 us -> 15.8 us  [swap(): return lax.ppermute(x, AXIS, [(i, i ^ mask) for i in range(count)])]
  transfers between devices with their start and end apart: 14 -> 14, of which waited for: 10 -> 7; matrix products, arithmetic and copies ran while one was open for 0% -> 0% of each run, Pallas kernels for 13% -> 13%
where the time goes in v5:
time: 28.8 us; the launch traced here: 28.6 us
  starting transfers between devices  15.8 us (55%)
  waiting for transfers between devices  6.08 us (21%)
  Pallas kernels  5.97 us (21%)
  between operations  0.73 us (3%)
    ppermute x14, starting transfers between devices, swap(): return lax.ppermute(x, AXIS, [(i, i ^ mask) for i in range(count)])  15.8 us
    ppermute x14, waiting for transfers between devices, swap(): return lax.ppermute(x, AXIS, [(i, i ^ mask) for i in range(count)])  6.08 us
    pallas_call x7, Pallas kernels, in_vmem(): pl.pallas_call(kernel, out_shape=out_shape, in_specs=[VMEM] * len(args),...  2.48 us
    pallas_call x2, Pallas kernels, final(): pl.pallas_call(lambda *refs: final_kernel(factor, work, *refs), out_shape...  2.19 us
    pallas_call x1, Pallas kernels, first_states(): pl.pallas_call(first_kernel, out_shape=(rows,) * 4 + (heads(4),), in_spec...  1.3 us
  transfers between devices with their start and end apart: 14, of which 7 were waited for; matrix products, arithmetic and copies ran while one was open for 0% of the time, Pallas kernels for 13%

profile of v5, /device:TPU:0, one launch (start us, length us, event | category | flops | bytes accessed | tf_op | source)
XLA Modules:
  0.0 28.6 jit_solution(2333766776334477969)
XLA Ops:
  0.6 1.3 %first_states.1 = (bf16[128,1024]{1,0:T(8,128)(2,1)S(1)}, bf16[128,1024]{1,0:T(8,128)(2,1)S(1)}, bf16[128,1024]{1,0:T(8,128)(2,1)S(1)}, bf16[128,1024]{1,0:T(8,128)(2,1)S(1)}, f32[4,128,128]{2,1,0:T(8,128)S(1)}) custom-call(bf16[128,1024]{1,0:T(8,128)(2,1)} %q_hbm.1, bf16[128,1024]{1,0:T(8,128)(2,1)} %k_hbm.1, bf16[128,1024]{1,0:T(8,128)(2,1)} %v_hbm.1, ...), custom_call_target="tpu_custom_call" | custom-call | tf_op jit(solution)/shard_map/first_states/pallas_call | solution.py:82
  1.9 0.5 %collective-permute-start = (f32[4,128,128]{2,1,0:T(8,128)S(1)}, f32[4,128,128]{2,1,0:T(8,128)S(1)}, u32[]{:S(2)}, u32[]{:S(2)}) collective-permute-start(f32[4,128,128]{2,1,0:T(8,128)S(1)} %get-tuple-element.34), channel_id=1, source_target_pairs={{0,1},{1,0},{2,3},{3,2},{4,5},{5,4},{6,7},{7,6},{8,9},{9,8},{10,11... | collective-permute-start | bytes 786440 | tf_op jit(solution)/shard_map/ppermute | solution.py:28
  2.5 0.4 %second_states.1 = (f32[4,128,128]{2,1,0:T(8,128)S(1)}, f32[4,128,128]{2,1,0:T(8,128)S(1)}, f32[4,128,128]{2,1,0:T(8,128)S(1)}) custom-call(bf16[128,1024]{1,0:T(8,128)(2,1)S(1)} %get-tuple-element.32.q_ref, bf16[128,1024]{1,0:T(8,128)(2,1)S(1)} %get-tuple-element.29.k_ref.refs_0_, bf16[128,1024]{1,0:T(8,128)(2,1)S(1)} %get-tuple-element.30.v_ref.refs_1_, ...), custom_call_target="tpu_custom_call" | custom-call | tf_op jit(solution)/shard_map/second_states/pallas_call | solution.py:44
  2.8 0.1 collective-permute-start.4
  3.0 0.7 %collective-permute-done.refs_10_ = f32[4,128,128]{2,1,0:T(8,128)S(1)} collective-permute-done((f32[4,128,128]{2,1,0:T(8,128)S(1)}, f32[4,128,128]{2,1,0:T(8,128)S(1)}, u32[]{:S(2)}, u32[]{:S(2)}) %collective-permute-start) | collective-permute-done | bytes 262176 | tf_op jit(solution)/shard_map/ppermute | solution.py:28
  3.7 4.0 %collective-permute-start.3 = (f32[128,128]{1,0:T(8,128)S(1)}, f32[128,128]{1,0:T(8,128)S(1)}, u32[]{:S(2)}, u32[]{:S(2)}) collective-permute-start(f32[128,128]{1,0:T(8,128)S(1)} %get-tuple-element.59), channel_id=1, source_target_pairs={{0,6},{1,7},{2,4},{3,5},{4,2},{5,3},{6,0},{7,1},{8,14},{9,15},{10,... | collective-permute-start | bytes 196616 | tf_op jit(solution)/shard_map/ppermute | solution.py:28
  7.6 0.4 %collective-permute-start.2 = (f32[128,128]{1,0:T(8,128)S(1)}, f32[128,128]{1,0:T(8,128)S(1)}, u32[]{:S(2)}, u32[]{:S(2)}) collective-permute-start(f32[128,128]{1,0:T(8,128)S(1)} %get-tuple-element.60), channel_id=1, source_target_pairs={{0,4},{1,5},{2,6},{3,7},{4,0},{5,1},{6,2},{7,3},{8,12},{9,13},{10,... | collective-permute-start | bytes 196616 | tf_op jit(solution)/shard_map/ppermute | solution.py:28
  8.1 0.2 collective-permute-start.1
  8.3 0.0 collective-permute-done.4.refs_11_
  8.3 1.9 %collective-permute-start.7 = (f32[128,128]{1,0:T(8,128)S(1)}, f32[128,128]{1,0:T(8,128)S(1)}, u32[]{:S(2)}, u32[]{:S(2)}) collective-permute-start(f32[128,128]{1,0:T(8,128)S(1)} %get-tuple-element.55), channel_id=1, source_target_pairs={{0,2},{1,3},{2,0},{3,1},{4,6},{5,7},{6,4},{7,5},{8,10},{9,11},{10,... | collective-permute-start | bytes 196616 | tf_op jit(solution)/shard_map/ppermute | solution.py:28
  10.2 1.5 %collective-permute-start.6 = (f32[128,128]{1,0:T(8,128)S(1)}, f32[128,128]{1,0:T(8,128)S(1)}, u32[]{:S(2)}, u32[]{:S(2)}) collective-permute-start(f32[128,128]{1,0:T(8,128)S(1)} %get-tuple-element.56), channel_id=1, source_target_pairs={{0,6},{1,7},{2,4},{3,5},{4,2},{5,3},{6,0},{7,1},{8,14},{9,15},{10,... | collective-permute-start | bytes 196616 | tf_op jit(solution)/shard_map/ppermute | solution.py:28
  11.7 0.0 collective-permute-done.3.refs_3_.refs_2_
  11.7 0.8 %collective-permute-start.5 = (f32[128,128]{1,0:T(8,128)S(1)}, f32[128,128]{1,0:T(8,128)S(1)}, u32[]{:S(2)}, u32[]{:S(2)}) collective-permute-start(f32[128,128]{1,0:T(8,128)S(1)} %get-tuple-element.57), channel_id=1, source_target_pairs={{0,4},{1,5},{2,6},{3,7},{4,0},{5,1},{6,2},{7,3},{8,12},{9,13},{10,... | collective-permute-start | bytes 196616 | tf_op jit(solution)/shard_map/ppermute | solution.py:28
  12.5 0.0 collective-permute-done.2.refs_2_.refs_1_
  12.5 0.0 collective-permute-done.1.refs_1_.refs_3_
  12.5 2.7 %collective-permute-start.8 = (f32[128,128]{1,0:T(8,128)S(1)}, f32[128,128]{1,0:T(8,128)S(1)}, u32[]{:S(2)}, u32[]{:S(2)}) collective-permute-start(f32[128,128]{1,0:T(8,128)S(1)} %sum_a.1), channel_id=1, source_target_pairs={{0,8},{1,9},{2,10},{3,11},{4,12},{5,13},{6,14},{7,15},{8,0},{9,1},... | collective-permute-start | bytes 196616 | tf_op jit(solution)/shard_map/ppermute | solution.py:28
  15.2 0.1 scan_a.1
  15.3 0.2 collective-permute-done.6.refs_6_
  15.4 0.6 %collective-permute-done.5.refs_5_ = f32[128,128]{1,0:T(8,128)S(1)} collective-permute-done((f32[128,128]{1,0:T(8,128)S(1)}, f32[128,128]{1,0:T(8,128)S(1)}, u32[]{:S(2)}, u32[]{:S(2)}) %collective-permute-start.5) | collective-permute-done | bytes 65568 | tf_op jit(solution)/shard_map/ppermute | solution.py:28
  16.0 1.9 %collective-permute-done.8.refs_8_ = f32[128,128]{1,0:T(8,128)S(1)} collective-permute-done((f32[128,128]{1,0:T(8,128)S(1)}, f32[128,128]{1,0:T(8,128)S(1)}, u32[]{:S(2)}, u32[]{:S(2)}) %collective-permute-start.8) | collective-permute-done | bytes 65568 | tf_op jit(solution)/shard_map/ppermute | solution.py:28
  17.9 0.1 scan_b.1
  18.0 1.5 %collective-permute-start.12 = (f32[2,128,128]{2,1,0:T(8,128)S(1)}, f32[2,128,128]{2,1,0:T(8,128)S(1)}, u32[]{:S(2)}, u32[]{:S(2)}) collective-permute-start(f32[2,128,128]{2,1,0:T(8,128)S(1)} %get-tuple-element.51), channel_id=1, source_target_pairs={{0,2},{1,3},{2,0},{3,1},{4,6},{5,7},{6,4},{7,5},{8,10},{9,11},{10,... | collective-permute-start | bytes 393224 | tf_op jit(solution)/shard_map/ppermute | solution.py:28
  19.5 1.6 %collective-permute-start.9 = (f32[2,128,128]{2,1,0:T(8,128)S(1)}, f32[2,128,128]{2,1,0:T(8,128)S(1)}, u32[]{:S(2)}, u32[]{:S(2)}) collective-permute-start(f32[2,128,128]{2,1,0:T(8,128)S(1)} %get-tuple-element.41), channel_id=1, source_target_pairs={{0,6},{1,7},{2,4},{3,5},{4,2},{5,3},{6,0},{7,1},{8,14},{9,15},{10,... | collective-permute-start | bytes 393224 | tf_op jit(solution)/shard_map/ppermute | solution.py:28
  21.1 0.4 %collective-permute-start.10 = (f32[2,128,128]{2,1,0:T(8,128)S(1)}, f32[2,128,128]{2,1,0:T(8,128)S(1)}, u32[]{:S(2)}, u32[]{:S(2)}) collective-permute-start(f32[2,128,128]{2,1,0:T(8,128)S(1)} %get-tuple-element.48), channel_id=1, source_target_pairs={{0,4},{1,5},{2,6},{3,7},{4,0},{5,1},{6,2},{7,3},{8,12},{9,13},{10,... | collective-permute-start | bytes 393224 | tf_op jit(solution)/shard_map/ppermute | solution.py:28
  21.5 1.9 %inner.1 = (f32[128,1024]{1,0:T(8,128)S(1)}, f32[128,1024]{1,0:T(8,128)S(1)}, f32[128,1024]{1,0:T(8,128)S(1)}) custom-call(bf16[128,1024]{1,0:T(8,128)(2,1)S(1)} %get-tuple-element.32.q_ref, bf16[128,1024]{1,0:T(8,128)(2,1)S(1)} %get-tuple-element.29.k_ref.refs_0_, bf16[128,1024]{1,0:T(8,128)(2,1)S(1)} %get-tuple-element.30.v_ref.refs_1_, ...), custom_call_target="tpu_custom_call" | custom-call | tf_op jit(solution)/shard_map/inner/pallas_call | solution.py:44
  23.5 0.1 collective-permute-start.13
  23.5 1.8 %collective-permute-done.9.refs_3_.refs_9_ = f32[2,128,128]{2,1,0:T(8,128)S(1)} collective-permute-done((f32[2,128,128]{2,1,0:T(8,128)S(1)}, f32[2,128,128]{2,1,0:T(8,128)S(1)}, u32[]{:S(2)}, u32[]{:S(2)}) %collective-permute-start.9) | collective-permute-done | bytes 131104 | tf_op jit(solution)/shard_map/ppermute | solution.py:28
  25.4 0.7 %collective-permute-done.10.refs_2_.refs_8_ = f32[2,128,128]{2,1,0:T(8,128)S(1)} collective-permute-done((f32[2,128,128]{2,1,0:T(8,128)S(1)}, f32[2,128,128]{2,1,0:T(8,128)S(1)}, u32[]{:S(2)}, u32[]{:S(2)}) %collective-permute-start.10) | collective-permute-done | bytes 131104 | tf_op jit(solution)/shard_map/ppermute | solution.py:28
  26.1 0.1 collective-permute-start.11
  26.2 1.3 %final.2 = (bf16[128,1024]{1,0:T(8,128)(2,1)}, bf16[128,1024]{1,0:T(8,128)(2,1)}, bf16[128,1024]{1,0:T(8,128)(2,1)}) custom-call(bf16[128,1024]{1,0:T(8,128)(2,1)S(1)} %get-tuple-element.29.k_ref.refs_0_, bf16[128,1024]{1,0:T(8,128)(2,1)S(1)} %get-tuple-element.30.v_ref.refs_1_, bf16[128,1024]{1,0:T(8,128)(2,1)S(1)} %get-tuple-element.31.g_ref.refs_2_, ...), custom_call_target="tpu_custom_call" | custom-call | tf_op jit(solution)/shard_map/final/pallas_call | solution.py:189
  27.5 0.2 collective-permute-done.11.refs_6_
  27.7 0.9 %final.3 = (bf16[128,1024]{1,0:T(8,128)(2,1)}, bf16[128,1024]{1,0:T(8,128)(2,1)}, bf16[128,1024]{1,0:T(8,128)(2,1)}) custom-call(bf16[128,1024]{1,0:T(8,128)(2,1)S(1)} %get-tuple-element.29.k_ref.refs_0_, bf16[128,1024]{1,0:T(8,128)(2,1)S(1)} %get-tuple-element.30.v_ref.refs_1_, ...), custom_call_target="tpu_custom_call", output_to_operand_aliasing={{0}: (7, {}), {1}: (8, {}), {2}: (9, {})} | custom-call | tf_op jit(solution)/shard_map/final/pallas_call | solution.py:189
  (8 shorter events, 0.2 us)
Async XLA Ops:
  1.9 1.7 %collective-permute-start = (f32[4,128,128]{2,1,0:T(8,128)S(1)}, f32[4,128,128]{2,1,0:T(8,128)S(1)}, u32[]{:S(2)}, u32[]{:S(2)}) collective-permute-start(f32[4,128,128]{2,1,0:T(8,128)S(1)} %get-tuple-element.34), channel_id=1, source_target_pairs={{0,1},{1,0},{2,3},{3,2},{4,5},{5,4},{6,7},{7,6},{8,9},{9,8},{10,11... | collective-permute-start | bytes 786440 | tf_op jit(solution)/shard_map/ppermute | solution.py:28
  2.8 5.4 %collective-permute-start.4 = (f32[4,128,128]{2,1,0:T(8,128)S(1)}, f32[4,128,128]{2,1,0:T(8,128)S(1)}, u32[]{:S(2)}, u32[]{:S(2)}) collective-permute-start(f32[4,128,128]{2,1,0:T(8,128)S(1)} %get-tuple-element.40), channel_id=1, source_target_pairs={{0,1},{1,0},{2,3},{3,2},{4,5},{5,4},{6,7},{7,6},{8,9},{9,8},{10,11... | collective-permute-start | bytes 786440 | tf_op jit(solution)/shard_map/ppermute | solution.py:28
  3.7 8.1 %collective-permute-start.3 = (f32[128,128]{1,0:T(8,128)S(1)}, f32[128,128]{1,0:T(8,128)S(1)}, u32[]{:S(2)}, u32[]{:S(2)}) collective-permute-start(f32[128,128]{1,0:T(8,128)S(1)} %get-tuple-element.59), channel_id=1, source_target_pairs={{0,6},{1,7},{2,4},{3,5},{4,2},{5,3},{6,0},{7,1},{8,14},{9,15},{10,... | collective-permute-start | bytes 196616 | tf_op jit(solution)/shard_map/ppermute | solution.py:28
  7.6 4.9 %collective-permute-start.2 = (f32[128,128]{1,0:T(8,128)S(1)}, f32[128,128]{1,0:T(8,128)S(1)}, u32[]{:S(2)}, u32[]{:S(2)}) collective-permute-start(f32[128,128]{1,0:T(8,128)S(1)} %get-tuple-element.60), channel_id=1, source_target_pairs={{0,4},{1,5},{2,6},{3,7},{4,0},{5,1},{6,2},{7,3},{8,12},{9,13},{10,... | collective-permute-start | bytes 196616 | tf_op jit(solution)/shard_map/ppermute | solution.py:28
  8.1 4.4 %collective-permute-start.1 = (f32[128,128]{1,0:T(8,128)S(1)}, f32[128,128]{1,0:T(8,128)S(1)}, u32[]{:S(2)}, u32[]{:S(2)}) collective-permute-start(f32[128,128]{1,0:T(8,128)S(1)} %get-tuple-element.61), channel_id=1, source_target_pairs={{0,2},{1,3},{2,0},{3,1},{4,6},{5,7},{6,4},{7,5},{8,10},{9,11},{10,... | collective-permute-start | bytes 196616 | tf_op jit(solution)/shard_map/ppermute | solution.py:28
  8.3 6.9 %collective-permute-start.7 = (f32[128,128]{1,0:T(8,128)S(1)}, f32[128,128]{1,0:T(8,128)S(1)}, u32[]{:S(2)}, u32[]{:S(2)}) collective-permute-start(f32[128,128]{1,0:T(8,128)S(1)} %get-tuple-element.55), channel_id=1, source_target_pairs={{0,2},{1,3},{2,0},{3,1},{4,6},{5,7},{6,4},{7,5},{8,10},{9,11},{10,... | collective-permute-start | bytes 196616 | tf_op jit(solution)/shard_map/ppermute | solution.py:28
  10.2 5.2 %collective-permute-start.6 = (f32[128,128]{1,0:T(8,128)S(1)}, f32[128,128]{1,0:T(8,128)S(1)}, u32[]{:S(2)}, u32[]{:S(2)}) collective-permute-start(f32[128,128]{1,0:T(8,128)S(1)} %get-tuple-element.56), channel_id=1, source_target_pairs={{0,6},{1,7},{2,4},{3,5},{4,2},{5,3},{6,0},{7,1},{8,14},{9,15},{10,... | collective-permute-start | bytes 196616 | tf_op jit(solution)/shard_map/ppermute | solution.py:28
  11.7 4.3 %collective-permute-start.5 = (f32[128,128]{1,0:T(8,128)S(1)}, f32[128,128]{1,0:T(8,128)S(1)}, u32[]{:S(2)}, u32[]{:S(2)}) collective-permute-start(f32[128,128]{1,0:T(8,128)S(1)} %get-tuple-element.57), channel_id=1, source_target_pairs={{0,4},{1,5},{2,6},{3,7},{4,0},{5,1},{6,2},{7,3},{8,12},{9,13},{10,... | collective-permute-start | bytes 196616 | tf_op jit(solution)/shard_map/ppermute | solution.py:28
  12.5 5.4 %collective-permute-start.8 = (f32[128,128]{1,0:T(8,128)S(1)}, f32[128,128]{1,0:T(8,128)S(1)}, u32[]{:S(2)}, u32[]{:S(2)}) collective-permute-start(f32[128,128]{1,0:T(8,128)S(1)} %sum_a.1), channel_id=1, source_target_pairs={{0,8},{1,9},{2,10},{3,11},{4,12},{5,13},{6,14},{7,15},{8,0},{9,1},... | collective-permute-start | bytes 196616 | tf_op jit(solution)/shard_map/ppermute | solution.py:28
  18.0 5.4 %collective-permute-start.12 = (f32[2,128,128]{2,1,0:T(8,128)S(1)}, f32[2,128,128]{2,1,0:T(8,128)S(1)}, u32[]{:S(2)}, u32[]{:S(2)}) collective-permute-start(f32[2,128,128]{2,1,0:T(8,128)S(1)} %get-tuple-element.51), channel_id=1, source_target_pairs={{0,2},{1,3},{2,0},{3,1},{4,6},{5,7},{6,4},{7,5},{8,10},{9,11},{10,... | collective-permute-start | bytes 393224 | tf_op jit(solution)/shard_map/ppermute | solution.py:28
  19.5 5.9 %collective-permute-start.9 = (f32[2,128,128]{2,1,0:T(8,128)S(1)}, f32[2,128,128]{2,1,0:T(8,128)S(1)}, u32[]{:S(2)}, u32[]{:S(2)}) collective-permute-start(f32[2,128,128]{2,1,0:T(8,128)S(1)} %get-tuple-element.41), channel_id=1, source_target_pairs={{0,6},{1,7},{2,4},{3,5},{4,2},{5,3},{6,0},{7,1},{8,14},{9,15},{10,... | collective-permute-start | bytes 393224 | tf_op jit(solution)/shard_map/ppermute | solution.py:28
  21.1 5.0 %collective-permute-start.10 = (f32[2,128,128]{2,1,0:T(8,128)S(1)}, f32[2,128,128]{2,1,0:T(8,128)S(1)}, u32[]{:S(2)}, u32[]{:S(2)}) collective-permute-start(f32[2,128,128]{2,1,0:T(8,128)S(1)} %get-tuple-element.48), channel_id=1, source_target_pairs={{0,4},{1,5},{2,6},{3,7},{4,0},{5,1},{6,2},{7,3},{8,12},{9,13},{10,... | collective-permute-start | bytes 393224 | tf_op jit(solution)/shard_map/ppermute | solution.py:28
  23.5 2.7 %collective-permute-start.13 = (f32[2,2,128,128]{3,2,1,0:T(8,128)S(1)}, f32[2,2,128,128]{3,2,1,0:T(8,128)S(1)}, u32[]{:S(2)}, u32[]{:S(2)}) collective-permute-start(f32[2,2,128,128]{3,2,1,0:T(8,128)S(1)} %pair.3), channel_id=1, source_target_pairs={{0,1},{1,0},{2,3},{3,2},{4,5},{5,4},{6,7},{7,6},{8,9},{9,8},{10,11... | collective-permute-start | bytes 786440 | tf_op jit(solution)/shard_map/ppermute | solution.py:28
  26.1 1.6 %collective-permute-start.11 = (f32[2,2,128,128]{3,2,1,0:T(8,128)S(1)}, f32[2,2,128,128]{3,2,1,0:T(8,128)S(1)}, u32[]{:S(2)}, u32[]{:S(2)}) collective-permute-start(f32[2,2,128,128]{3,2,1,0:T(8,128)S(1)} %pair.2), channel_id=1, source_target_pairs={{0,1},{1,0},{2,3},{3,2},{4,5},{5,4},{6,7},{7,6},{8,9},{9,8},{10,11... | collective-permute-start | bytes 786440 | tf_op jit(solution)/shard_map/ppermute | solution.py:28
